TPU v7x, 512 devices: a whole 4x4x16 slice. The times are simulated.
512 devices in a mesh: src: 32 (over z, core), tgt: 16 (over y, x).
Axes of the slice: x: 4, y: 4, z: 16, core: 2. Of those that a mesh axis runs over, the one named last changes fastest.
Arguments:
- source_embed: bfloat16 [512, 128, 128], P('src', None, 'tgt'), may hold values from -4 to 4
- target_embed: bfloat16 [256, 128, 128], P('tgt', None, 'src'), may hold values from -4 to 4
- source_mass: float32 [512, 128], P('src'), may hold values from 10 to 14
- target_mass: float32 [256, 128], P('tgt'), may hold values from 10 to 14
- target_start: float32 [256, 128], P('tgt'), may hold values from -6 to 6
- block_pairs: int32 [32, 16, 128, 2], P('src', 'tgt'), may hold values from 0 to 15, as said below
- counts: int32 [32, 16], P('src', 'tgt'), may hold values from 16 to 128, as said below
Outputs:
- sender_log_scaling: float32 [512, 128], P('src')
- target_dual_potential: float32 [256, 128], P('tgt')
Inputs may be any that keep to these rules, and one draw needn't show every extreme that they name: `block_pairs`: entry 0 of a slot is a local source block (below 16), entry 1 a local target block (below 16). The live slots of a device name distinct pairs; its first 16 slots name each of its target blocks once and each of its source blocks at least once. Slots at or past the device's count are not kept and hold arbitrary block numbers. `counts`: some device has all 128 slots live in every draw.
All inputs are finite; a program needn't handle non-finite values.
Results may differ from a plain program's by a relative error of at most 0.0003.
Values may be sent and summed in bfloat16 or wider, within the bound.
No kernel may reach another device: no remote copies, remote signals or barrier semaphores. Data moves between devices by JAX's collectives and lax.ppermute only.
A program may use at most 64 MiB of HBM per device.

v0:
```python
import jax
import jax.numpy as jnp
from jax import lax
from jax.sharding import Mesh
from jax.sharding import PartitionSpec as P

ITERS = 2
SRC = ("src_0", "src_1")


smoothing_epsilon = 4.0
empty_peak = -1e30
slot_batch = 8


def from_everyone(x, axis):
    length = lax.axis_size(axis)
    return lax.all_to_all(jnp.broadcast_to(x[None], (length, *x.shape)), axis, 0, 0, tiled=True)


def gathered_once(x, axis):
    leaves = jax.tree.leaves(x)
    order = sorted(range(len(leaves)), key=lambda k: -leaves[k].size)
    width = (1, *leaves[order[0]].shape)[-1]
    lines = [
        jnp.pad(leaves[k].reshape(-1), (0, -leaves[k].size % width)).reshape(-1, width)
        for k in order
    ]
    both, at, found = (from_everyone(jnp.concatenate(lines), axis), 0, {})
    for k, line in zip(order, lines):
        slab = both[:, at : at + len(line)].reshape(len(both), -1)
        found[k] = slab[:, : leaves[k].size].reshape(-1, *leaves[k].shape)
        at += len(line)
    numbers = iter(range(len(leaves)))
    return jax.tree.map(lambda _: found[next(numbers)], x)


def folded_in_pairs(pieces, combine):
    while len(jax.tree.leaves(pieces)[0]) > 1:
        pieces = jax.vmap(combine)(
            *(jax.tree.map(lambda part: part[side::2], pieces) for side in (0, 1))
        )
    return jax.tree.map(lambda part: part[0], pieces)


def combined_all(x, axis, combine):
    pieces = gathered_once(x, axis)
    return folded_in_pairs(pieces, combine)


def all_in_one(x, axis):
    leaves = jax.tree.leaves(x)
    order = sorted(range(len(leaves)), key=lambda k: -leaves[k].size)
    width = (1, *leaves[order[0]].shape)[-1]
    lines = [
        jnp.pad(leaves[k].reshape(-1), (0, -leaves[k].size % width)).reshape(-1, width)
        for k in order
    ]
    both, at, found = (lax.all_gather(jnp.concatenate(lines), axis), 0, {})
    for k, line in zip(order, lines):
        slab = both[:, at : at + len(line)].reshape(len(both), -1)
        found[k] = slab[:, : leaves[k].size].reshape(-1, *leaves[k].shape)
        at += len(line)
    numbers = iter(range(len(leaves)))
    return jax.tree.map(lambda _: found[next(numbers)], x)


def combined_by_axis(x, axes, combine):
    for axis in axes:
        pieces = all_in_one(x, axis)
        x = jax.tree.map(lambda part: part[0], pieces)
        for k in range(1, lax.axis_size(axis)):
            x = combine(x, jax.tree.map(lambda part: part[k], pieces))
    return x


def laid_out(pieces, dim):
    lengths = list(pieces.shape[1:])
    lengths[dim] *= pieces.shape[0]
    return jnp.moveaxis(pieces, 0, dim).reshape(lengths)


def gather_directly(x, axis, dim):
    return laid_out(from_everyone(x, axis), dim)


def absorb(maxima, totals, targets, block_peak, block_total):
    raised = maxima.at[targets].max(block_peak)
    totals = totals * jnp.exp(maxima - raised)
    totals = totals.at[targets].add(block_total * jnp.exp(block_peak - raised[targets]))
    return (raised, totals)


def combine_stats(first_pair, second_pair):
    joined = jnp.maximum(first_pair[0], second_pair[0])
    merged_sum = first_pair[1] * jnp.exp(first_pair[0] - joined) + second_pair[1] * jnp.exp(
        second_pair[0] - joined
    )
    return (joined, merged_sum)


def blank(blocks, frames):
    return (
        jnp.full((blocks, frames), empty_peak, jnp.float32),
        jnp.zeros((blocks, frames), jnp.float32),
    )


def block_stats(
    local_side, far_side, potential, slot_plan, column, first_slot, final_position_entry, running
):
    slot_count = slot_plan.shape[0]

    def group(counter, current):
        maxima, totals = current
        slot_ids = first_slot + counter * slot_batch + lax.iota(jnp.int32, slot_batch)
        usable = slot_ids < final_position_entry
        slot_ids = jnp.minimum(slot_ids, slot_count - 1)
        near = slot_plan[slot_ids, column]
        distant = slot_plan[slot_ids, 1 - column]
        similarity_matrix = (
            jnp.einsum(
                "fdg,fwg->fdw",
                local_side[near],
                far_side[distant],
                preferred_element_type=jnp.float32,
            )
            / smoothing_epsilon
        )
        similarity_matrix = similarity_matrix + potential[distant][:, None, :]
        block_peak = jnp.max(similarity_matrix, axis=2)
        block_total = jnp.sum(jnp.exp(similarity_matrix - block_peak[:, :, None]), axis=2)
        block_peak = jnp.where(usable[:, None], block_peak, empty_peak)
        block_total = jnp.where(usable[:, None], block_total, 0.0)
        return absorb(maxima, totals, near, block_peak, block_total)

    groups = jnp.maximum(final_position_entry - first_slot + slot_batch - 1, 0) // slot_batch
    return lax.fori_loop(0, groups, group, running)


def fold_rows(running):
    result = combined_all(running, "tgt", combine_stats)
    return result


def collapse_columns(running):
    result = combined_by_axis(running, SRC, combine_stats)
    return result


def finish(log_mass, running):
    return log_mass - (running[0] + jnp.log(running[1]))


def on_device(
    source_embed, target_embed, source_mass, target_mass, target_start, block_pairs, counts
):
    source_full = gather_directly(source_embed, "tgt", 2)
    target_full = gather_directly(target_embed, SRC, 2)
    slot_plan = block_pairs.reshape(block_pairs.shape[2], 2)
    live_count = counts.reshape(())
    source_blocks = source_full.shape[0]
    target_blocks = target_full.shape[0]
    frames = source_full.shape[1]
    target_dual_potential = target_start
    sender_log_scaling = source_mass
    for iteration in range(ITERS):
        running = block_stats(
            source_full,
            target_full,
            target_dual_potential,
            slot_plan,
            0,
            0,
            live_count,
            blank(source_blocks, frames),
        )
        sender_log_scaling = finish(source_mass, fold_rows(running))
        running = block_stats(
            target_full,
            source_full,
            sender_log_scaling,
            slot_plan,
            1,
            0,
            live_count,
            blank(target_blocks, frames),
        )
        target_dual_potential = finish(target_mass, collapse_columns(running))
    return (sender_log_scaling, target_dual_potential)


def solution(mesh):
    split = Mesh(mesh.devices.reshape(16, 2, mesh.shape["tgt"]), ("src_0", "src_1", "tgt"))
    placed = (
        P(SRC, None, "tgt"),
        P("tgt", None, SRC),
        P(SRC, None),
        P("tgt", None),
        P("tgt", None),
        P(SRC, "tgt", None, None),
        P(SRC, "tgt"),
    )
    return jax.shard_map(
        on_device,
        mesh=split,
        in_specs=placed,
        out_specs=(P(SRC, None), P("tgt", None)),
        check_vma=False,
    )
```

profile of v0, /device:TPU:17, one launch (start us, length us, event | category | flops | bytes accessed | tf_op | source)
XLA Modules:
  0.0 515.2 jit_solution(17645497292154310239)
XLA Ops:
  0.6 1.6 broadcast_in_dim.104
  2.3 6.9 %all-to-all-start = ((bf16[16,16,128,8]{2,3,1,0:T(8,128)(2,1)}), bf16[16,16,128,8]{2,3,1,0:T(8,128)(2,1)S(1)}, u32[]{:S(2)}, u32[]{:S(2)}) async-start(bf16[16,16,128,8]{2,3,1,0:T(8,128)(2,1)} %broadcast_in_dim.104), calls=%async_computation | async-start | bytes 1048576 | tf_op jit(solution)/shard_map/all_to_all | solution.py:18
  9.2 6.7 %all-to-all-done = bf16[16,16,128,8]{2,3,1,0:T(8,128)(2,1)S(1)} async-done(((bf16[16,16,128,8]{2,3,1,0:T(8,128)(2,1)}), bf16[16,16,128,8]{2,3,1,0:T(8,128)(2,1)S(1)}, u32[]{:S(2)}, u32[]{:S(2)}) %all-to-all-start) | async-done | bytes 524320 | tf_op jit(solution)/shard_map/all_to_all | solution.py:18
  15.9 0.9 broadcast_in_dim.105
  16.8 18.7 %all-to-all-start.1 = ((bf16[32,16,128,4]{2,1,3,0:T(8,128)(2,1)}), bf16[32,16,128,4]{2,1,3,0:T(8,128)(2,1)S(1)}, u32[]{:S(2)}, u32[]{:S(2)}) async-start(bf16[32,16,128,4]{2,1,3,0:T(8,128)(2,1)} %broadcast_in_dim.105), calls=%async_computation.1 | async-start | bytes 1048576 | tf_op jit(solution)/shard_map/all_to_all | solution.py:18
  36.6 32.4 %all-to-all-done.1 = bf16[32,16,128,4]{2,1,3,0:T(8,128)(2,1)S(1)} async-done(((bf16[32,16,128,4]{2,1,3,0:T(8,128)(2,1)}), bf16[32,16,128,4]{2,1,3,0:T(8,128)(2,1)S(1)}, u32[]{:S(2)}, u32[]{:S(2)}) %all-to-all-start.1) | async-done | bytes 524320 | tf_op jit(solution)/shard_map/all_to_all | solution.py:18
  70.2 22.7 %while.48 = (s32[]{:T(128)}, f32[16,128]{1,0:T(8,128)S(1)}, f32[16,128]{1,0:T(8,128)S(1)}, s32[]{:T(128)}, s32[128,2]{0,1:T(2,128)S(1)}, /*index=5*/s32[]{:T(128...) while((s32[]{:T(128)}, f32[16,128]{1,0:T(8,128)S(1)}, ...), condition=%wide.region_5.6_spmd, body=%wide.region_0.5_spmd.sunk | while | flops 34221184 | bytes 2762505 | solution.py:138
  75.1 0.7 scatter_custom_fusion.35
  80.8 0.7 scatter_custom_fusion.35
  86.4 0.7 scatter_custom_fusion.35
  92.1 0.7 scatter_custom_fusion.35
  92.8 0.7 broadcast_in_dim.106
  93.6 61.0 %all-to-all-start.2 = ((f32[16,32,128]{2,1,0:T(8,128)}), f32[16,32,128]{2,1,0:T(8,128)S(1)}, u32[]{:S(2)}, u32[]{:S(2)}) async-start(f32[16,32,128]{2,1,0:T(8,128)} %broadcast_in_dim.106), calls=%async_computation.2 | async-start | bytes 524288 | tf_op jit(solution)/shard_map/all_to_all | solution.py:18
  154.5 5.2 %all-to-all-done.2 = f32[16,32,128]{2,1,0:T(8,128)S(1)} async-done(((f32[16,32,128]{2,1,0:T(8,128)}), f32[16,32,128]{2,1,0:T(8,128)S(1)}, u32[]{:S(2)}, u32[]{:S(2)}) %all-to-all-start.2) | async-done | bytes 262176 | tf_op jit(solution)/shard_map/all_to_all | solution.py:18
  160.6 22.7 %while.49 = (s32[]{:T(128)}, f32[16,128]{1,0:T(8,128)S(1)}, f32[16,128]{1,0:T(8,128)S(1)}, s32[]{:T(128)}, s32[128,2]{0,1:T(2,128)S(1)}, /*index=5*/s32[]{:T(128...) while((s32[]{:T(128)}, f32[16,128]{1,0:T(8,128)S(1)}, ...), condition=%wide.region_11.12_spmd, body=%wide.region_6.11_spmd.sunk | while | flops 34221184 | bytes 2762505 | solution.py:138
  165.5 0.7 scatter_custom_fusion.39
  171.2 0.7 scatter_custom_fusion.39
  176.9 0.7 scatter_custom_fusion.39
  182.5 0.7 scatter_custom_fusion.39
  183.3 71.4 %all-gather = f32[512,128]{1,0:T(8,128)S(1)} all-gather(f32[32,128]{1,0:T(8,128)S(1)} %pad_maximum_fusion.1), channel_id=2, replica_groups=mesh['src_0'=16,'src_1'=2,'tgt'=16] {'src_0'}, dimensions={0}, use_global_device_ids=true | all-gather | bytes 278528 | tf_op jit(solution)/shard_map/all_gather | solution.py:59
  254.7 38.9 %all-gather.1 = f32[64,128]{1,0:T(8,128)S(1)} all-gather(f32[32,128]{1,0:T(8,128)S(1)} %pad_maximum_fusion.2), channel_id=3, replica_groups=mesh['src_0'=16,'src_1'=2,'tgt'=16] {'src_1'}, dimensions={0}, use_global_device_ids=true | all-gather | bytes 49152 | tf_op jit(solution)/shard_map/all_gather | solution.py:59
  293.6 22.7 %while.50 = (s32[]{:T(128)}, f32[16,128]{1,0:T(8,128)S(1)}, f32[16,128]{1,0:T(8,128)S(1)}, s32[]{:T(128)}, s32[128,2]{0,1:T(2,128)S(1)}, /*index=5*/s32[]{:T(128...) while((s32[]{:T(128)}, f32[16,128]{1,0:T(8,128)S(1)}, ...), condition=%wide.region_17.18_spmd, body=%wide.region_12.17_spmd.sunk | while | flops 34221184 | bytes 2762505 | solution.py:138
  298.6 0.7 scatter_custom_fusion.43
  304.3 0.7 scatter_custom_fusion.43
  309.9 0.7 scatter_custom_fusion.43
  315.6 0.7 scatter_custom_fusion.43
  316.4 61.8 %all_to_all.20 = f32[16,32,128]{2,1,0:T(8,128)S(1)} all-to-all(f32[16,32,128]{2,1,0:T(8,128)S(1)} %broadcast_in_dim.107), channel_id=1, replica_groups=mesh['src_0'=16,'src_1'=2,'tgt'=16] {'tgt'}, dimensions={0} | all-to-all | bytes 524288 | tf_op jit(solution)/shard_map/all_to_all | solution.py:18
  378.3 22.7 %while.51 = (s32[]{:T(128)}, f32[16,128]{1,0:T(8,128)S(1)}, f32[16,128]{1,0:T(8,128)S(1)}, s32[]{:T(128)}, s32[128,2]{0,1:T(2,128)S(1)}, /*index=5*/s32[]{:T(128...) while((s32[]{:T(128)}, f32[16,128]{1,0:T(8,128)S(1)}, ...), condition=%wide.region_23.24_spmd, body=%wide.region_18.23_spmd.sunk | while | flops 34221184 | bytes 2762505 | solution.py:138
  383.2 0.7 scatter_custom_fusion.47
  388.9 0.7 scatter_custom_fusion.47
  401.6 66.5 %all-gather.2 = f32[512,128]{1,0:T(8,128)S(1)} all-gather(f32[32,128]{1,0:T(8,128)S(1)} %pad_maximum_fusion.4), channel_id=4, replica_groups=mesh['src_0'=16,'src_1'=2,'tgt'=16] {'src_0'}, dimensions={0}, use_global_device_ids=true | all-gather | bytes 278528 | tf_op jit(solution)/shard_map/all_gather | solution.py:59
  468.2 46.4 %all-gather.3 = f32[64,128]{1,0:T(8,128)S(1)} all-gather(f32[32,128]{1,0:T(8,128)S(1)} %pad_maximum_fusion.5), channel_id=5, replica_groups=mesh['src_0'=16,'src_1'=2,'tgt'=16] {'src_1'}, dimensions={0}, use_global_device_ids=true | all-gather | bytes 49152 | tf_op jit(solution)/shard_map/all_gather | solution.py:59
  (319 shorter events, 82.9 us)
Async XLA Ops:
  2.3 6.9 %copy-start.5 = (bf16[16,128,4]{1,2,0:T(4,128)(2,1)S(1)}, bf16[16,128,4]{1,2,0:T(4,128)(2,1)}, u32[]{:S(2)}) copy-start(bf16[16,128,4]{1,2,0:T(4,128)(2,1)} %param.16) | copy-start | bytes 49156
  2.3 13.6 %all-to-all-start = ((bf16[16,16,128,8]{2,3,1,0:T(8,128)(2,1)}), bf16[16,16,128,8]{2,3,1,0:T(8,128)(2,1)S(1)}, u32[]{:S(2)}, u32[]{:S(2)}) async-start(bf16[16,16,128,8]{2,3,1,0:T(8,128)(2,1)} %broadcast_in_dim.104), calls=%async_computation | async-start | bytes 1048576 | tf_op jit(solution)/shard_map/all_to_all | solution.py:18
  16.8 52.2 %all-to-all-start.1 = ((bf16[32,16,128,4]{2,1,3,0:T(8,128)(2,1)}), bf16[32,16,128,4]{2,1,3,0:T(8,128)(2,1)S(1)}, u32[]{:S(2)}, u32[]{:S(2)}) async-start(bf16[32,16,128,4]{2,1,3,0:T(8,128)(2,1)} %broadcast_in_dim.105), calls=%async_computation.1 | async-start | bytes 1048576 | tf_op jit(solution)/shard_map/all_to_all | solution.py:18
  69.5 0.7 copy-start.2
  69.5 0.7 copy-start
  93.6 66.2 %all-to-all-start.2 = ((f32[16,32,128]{2,1,0:T(8,128)}), f32[16,32,128]{2,1,0:T(8,128)S(1)}, u32[]{:S(2)}, u32[]{:S(2)}) async-start(f32[16,32,128]{2,1,0:T(8,128)} %broadcast_in_dim.106), calls=%async_computation.2 | async-start | bytes 524288 | tf_op jit(solution)/shard_map/all_to_all | solution.py:18
  159.8 0.7 copy-start.3
  254.7 38.9 %copy-start.4 = (f32[16,128]{1,0:T(8,128)S(1)}, f32[16,128]{1,0:T(8,128)}, u32[]{:S(2)}) copy-start(f32[16,128]{1,0:T(8,128)} %param.18) | copy-start | bytes 24580
  401.0 0.6 copy-start.1
where the time goes:
time: 520 us; the launch traced here: 515 us
  blocking collectives  285 us (55%)
  starting transfers between devices  86.5 us (17%)
  local copies, waits for them, and re-layouts  55.3 us (11%)
  waiting for transfers between devices  44.4 us (9%)
  other arithmetic  35.6 us (7%)
    all_gather x4, blocking collectives, all_in_one(): both, at, found = (lax.all_gather(jnp.concatenate(lines), axis), 0, {})  223 us
    all_to_all x3, starting transfers between devices, from_everyone(): lax.all_to_all(jnp.broadcast_to(x[None], (length, *x.shape)), axis, 0, 0,...  86.5 us
    all_to_all x1, blocking collectives, from_everyone(): lax.all_to_all(jnp.broadcast_to(x[None], (length, *x.shape)), axis, 0, 0,...  61.8 us
    all_to_all x3, waiting for transfers between devices, from_everyone(): lax.all_to_all(jnp.broadcast_to(x[None], (length, *x.shape)), axis, 0, 0,...  44.4 us
    scatter-add x16, other arithmetic, absorb(): totals.at[targets].add(block_total * jnp.exp(block_peak - raised[targets]))  11.1 us
    another operation x16, other arithmetic, absorb(): raised = maxima.at[targets].max(block_peak)  10.9 us
    gather x16, local copies, waits for them, and re-layouts, group(): near = slot_plan[slot_ids, column]  10.5 us
    gather x16, local copies, waits for them, and re-layouts, group(): distant = slot_plan[slot_ids, 1 - column]  10.5 us
  transfers between devices with their start and end apart: 3, of which 3 were waited for; matrix products, arithmetic and copies ran while one was open for 0% of the time, Pallas kernels for 0%

commit v1 on v0

v1 whole, which is shorter than its diff:
```python
import functools
import math

import jax
import jax.numpy as jnp
from jax import lax
from jax.experimental import pallas as pl
from jax.experimental.pallas import tpu as pltpu
from jax.sharding import Mesh
from jax.sharding import PartitionSpec as P

ITERS = 2
SRC = ("z", "c")

smoothing_epsilon = 4.0
empty_peak = -1e30
log2e = 1.0 / math.log(2.0)
to_log2 = log2e / smoothing_epsilon
group = 4
pot_most = 20.0
sum_least = 4.3e-18
sum_most = 5e34


def log_sum_exp(pieces):
    peak = functools.reduce(jnp.maximum, pieces)
    total = functools.reduce(jnp.add, [jnp.exp(piece - peak) for piece in pieces])
    return peak + jnp.log(total)


def scores(rows, columns):
    return lax.dot_general(
        rows, columns, (((1,), (0,)), ((), ())), preferred_element_type=jnp.float32
    )


def over_slots(count, body):
    whole = count // group

    @pl.loop(0, whole)
    def _(step):
        for lane in range(group):
            body(step * group + lane)

    @pl.loop(whole * group, count)
    def _(slot):
        body(slot)


def within(potential, sums):
    fine = (
        (jnp.abs(potential) <= pot_most) & (sums >= sum_least) & (sums <= sum_most)
    )
    return jnp.min(jnp.where(fine, 1.0, 0.0)) > 0.5


def rows_kept(sums, row_of):
    for block in range(sums.shape[0]):
        sums[block : block + 1, :] = row_of(block)


def exact_rows(count, pairs, rows, columns, potential, peak, total, sums):
    peak[...] = jnp.full_like(peak, empty_peak)
    total[...] = jnp.zeros_like(total)

    @pl.loop(0, count)
    def _(slot):
        source, target = pairs[0, slot], pairs[1, slot]
        value = scores(rows[source], columns[target]) * to_log2
        value = value + potential[pl.ds(target, 1), :] * log2e
        raised = jnp.maximum(peak[source], value)
        total[source] = total[source] * jnp.exp2(peak[source] - raised) + jnp.exp2(
            value - raised
        )
        peak[source] = raised

    def one(block):
        tall, across = peak[block].T, total[block].T
        most = jnp.max(tall, axis=0, keepdims=True)
        summed = jnp.sum(across * jnp.exp2(tall - most), axis=0, keepdims=True)
        return most / log2e + jnp.log(summed)

    rows_kept(sums, one)


def exact_columns(count, pairs, rows, columns, potential, wide, peak, total, sums):
    peak[...] = jnp.full_like(peak, empty_peak)
    total[...] = jnp.zeros_like(total)
    for block in range(wide.shape[0]):
        wide[block] = jnp.broadcast_to(potential[block : block + 1, :], wide.shape[1:]).T

    @pl.loop(0, count)
    def _(slot):
        source, target = pairs[0, slot], pairs[1, slot]
        value = scores(rows[source], columns[target]) * to_log2
        value = value + wide[source] * log2e
        raised = jnp.maximum(peak[target], value)
        total[target] = total[target] * jnp.exp2(peak[target] - raised) + jnp.exp2(
            value - raised
        )
        peak[target] = raised

    def one(block):
        most = jnp.max(peak[block], axis=0, keepdims=True)
        summed = jnp.sum(total[block] * jnp.exp2(peak[block] - most), axis=0, keepdims=True)
        return most / log2e + jnp.log(summed)

    rows_kept(sums, one)


def spread(partial, sums):
    partial[...] = jnp.broadcast_to(sums[...][None], partial.shape)


def row_pass(count, pairs, rows, columns, potential, kernel_of, weights, total, peak, sums, partial):
    weights[...] = jnp.exp(potential[...])
    total[...] = jnp.zeros_like(total)

    def body(slot):
        source, target = pairs[0, slot], pairs[1, slot]
        total[source] = total[source] + kernel_of(slot, source, target) * weights[
            pl.ds(target, 1), :
        ]

    over_slots(count, body)
    rows_kept(sums, lambda block: jnp.sum(total[block].T, axis=0, keepdims=True))
    fine = within(potential[...], sums[...])

    @pl.when(fine)
    def _():
        sums[...] = jnp.log(sums[...])

    @pl.when(jnp.logical_not(fine))
    def _():
        exact_rows(count, pairs, rows, columns, potential, peak, total, sums)

    spread(partial, sums)


def first_kernel(
    count_ref, pairs, source, target, start, cached, rows, columns, partial,
    wide_source, wide_target, weights, total, peak, sums,
):
    blocks = source.shape[1]
    features = source.shape[2]
    for device in range(source.shape[0]):
        wide_source[:, pl.ds(device * features, features), :] = source[device].astype(
            jnp.float32
        )
    cores, rings, _, parts, _ = target.shape
    for ring in range(rings):
        for core in range(cores):
            at = (ring * cores + core) * parts
            wide_target[:, pl.ds(at, parts), :] = target[core, ring].astype(jnp.float32)
    for block in range(blocks):
        rows[block] = wide_source[block].T.astype(jnp.bfloat16)
        columns[block] = wide_target[block].astype(jnp.bfloat16)

    def kernel_of(slot, source, target):
        value = jnp.exp2(scores(rows[source], columns[target]) * to_log2)
        cached[slot] = value
        return value

    row_pass(
        count_ref[0], pairs, rows, columns, start, kernel_of, weights, total, peak, sums, partial
    )


def column_kernel(
    count_ref, pairs, cached, rows, columns, gathered, mass, scaling, partial,
    wide, slim, total, peak, sums,
):
    count = count_ref[0]
    scaling[...] = mass[...] - log_sum_exp([gathered[k] for k in range(gathered.shape[0])])
    weights = jnp.exp(scaling[...])
    for block in range(wide.shape[0]):
        wide[block] = jnp.broadcast_to(weights[block : block + 1, :], wide.shape[1:]).T
    slim[...] = jnp.zeros_like(slim)

    def body(slot):
        source, target = pairs[0, slot], pairs[1, slot]
        value = cached[slot] * wide[source]
        value = value.reshape(-1, 8, value.shape[-1])
        slim[target] = slim[target] + jnp.sum(value, axis=0)

    over_slots(count, body)
    rows_kept(sums, lambda block: jnp.sum(slim[block], axis=0, keepdims=True))
    fine = within(scaling[...], sums[...])

    @pl.when(fine)
    def _():
        sums[...] = jnp.log(sums[...])

    @pl.when(jnp.logical_not(fine))
    def _():
        exact_columns(count, pairs, rows, columns, scaling, wide, peak, total, sums)

    partial[...] = sums[...]


def row_kernel(
    count_ref, pairs, cached, rows, columns, gathered, mass, partial,
    potential, weights, total, peak, sums,
):
    potential[...] = mass[...] - log_sum_exp([gathered[k] for k in range(gathered.shape[0])])
    row_pass(
        count_ref[0], pairs, rows, columns, potential,
        lambda slot, source, target: cached[slot],
        weights, total, peak, sums, partial,
    )


def called(body, outs, scratch, *operands):
    smem = pl.BlockSpec(memory_space=pltpu.SMEM)
    vmem = pl.BlockSpec(memory_space=pltpu.VMEM)
    return pl.pallas_call(
        body,
        out_shape=outs,
        in_specs=[smem, smem] + [vmem] * (len(operands) - 2),
        out_specs=[vmem] * len(outs),
        scratch_shapes=scratch,
        compiler_params=pltpu.CompilerParams(vmem_limit_bytes=40 * 1024 * 1024),
    )(*operands)


def copies(x, axis):
    return jnp.broadcast_to(x[None], (lax.axis_size(axis), *x.shape))


def exchanged(x, axis):
    return lax.all_to_all(x, axis, 0, 0, tiled=True)


def on_device(
    source_embed, target_embed, source_mass, target_mass, target_start, block_pairs, counts
):
    f32, bf16 = jnp.float32, jnp.bfloat16
    slots = block_pairs.shape[2]
    pairs = block_pairs.reshape(slots, 2).T
    count = counts.reshape(1)
    source_blocks, frames, _ = source_embed.shape
    target_blocks = target_embed.shape[0]
    columns_gathered = exchanged(copies(jnp.swapaxes(target_embed, 1, 2), "z"), "z")
    source = exchanged(copies(jnp.swapaxes(source_embed, 1, 2), "tgt"), "tgt")
    target = lax.all_gather(columns_gathered, "c")
    across = lax.axis_size("tgt")
    features = across * source_embed.shape[2]
    line = jax.ShapeDtypeStruct((source_blocks, frames), f32)
    many = jax.ShapeDtypeStruct((across, source_blocks, frames), f32)
    square = pltpu.VMEM((source_blocks, frames, frames), f32)
    flat = pltpu.VMEM((source_blocks, frames), f32)
    cached, rows, columns, partial = called(
        first_kernel,
        [
            pltpu.VMEM((slots, frames, frames), f32),
            pltpu.VMEM((source_blocks, frames, features), bf16),
            pltpu.VMEM((target_blocks, features, frames), bf16),
            many,
        ],
        [
            pltpu.VMEM((source_blocks, features, frames), f32),
            pltpu.VMEM((target_blocks, features, frames), f32),
            flat, square, square, flat,
        ],
        count, pairs, source, target, target_start,
    )
    kept = [count, pairs]
    kept += [pltpu.with_memory_space_constraint(x, pltpu.VMEM) for x in (cached, rows, columns)]
    for iteration in range(ITERS):
        scaling, partial = called(
            column_kernel,
            [line, line],
            [square, pltpu.VMEM((target_blocks, 8, frames), f32), square, square, flat],
            *kept, exchanged(partial, "tgt"), source_mass,
        )
        both = lax.all_gather(partial, "c")
        merged = log_sum_exp([both[0], both[1]])
        gathered = exchanged(copies(merged, "z"), "z")
        if iteration < ITERS - 1:
            (partial,) = called(
                row_kernel,
                [many],
                [flat, flat, square, square, flat],
                *kept, gathered, target_mass,
            )
    potential = target_mass - log_sum_exp([gathered[k] for k in range(gathered.shape[0])])
    return scaling, potential


def solution(mesh):
    split = Mesh(mesh.devices.reshape(16, 2, mesh.shape["tgt"]), ("z", "c", "tgt"))
    placed = (
        P(SRC, None, "tgt"),
        P("tgt", None, SRC),
        P(SRC, None),
        P("tgt", None),
        P("tgt", None),
        P(SRC, "tgt", None, None),
        P(SRC, "tgt"),
    )
    return jax.shard_map(
        on_device,
        mesh=split,
        in_specs=placed,
        out_specs=(P(SRC, None), P("tgt", None)),
        check_vma=False,
    )
```

time: 520 us -> 180 us (0.35)
  the two profiles are of different devices: /device:TPU:17 before, /device:TPU:32 now
where the time goes in v1:
time: 180 us; the launch traced here: 179 us
  blocking collectives  143 us (79%)
  Pallas kernels  13.7 us (8%)
  waiting for transfers between devices  7.66 us (4%)
  starting transfers between devices  7.03 us (4%)
  local copies, waits for them, and re-layouts  5.46 us (3%)
    all_to_all x5, blocking collectives, exchanged(): return lax.all_to_all(x, axis, 0, 0, tiled=True)  137 us
    pallas_call x4, Pallas kernels, called(): pl.pallas_call(body, out_shape=outs, in_specs=[smem, smem] + [vmem] * (le...  13.7 us
    all_to_all x1, waiting for transfers between devices, exchanged(): return lax.all_to_all(x, axis, 0, 0, tiled=True)  7.66 us
    all_to_all x1, starting transfers between devices, exchanged(): return lax.all_to_all(x, axis, 0, 0, tiled=True)  7.03 us
    all_gather x2, blocking collectives, on_device(): both = lax.all_gather(partial, 'c')  3.6 us
  transfers between devices with their start and end apart: 1, of which 1 were waited for; matrix products, arithmetic and copies ran while one was open for 0% of the time, Pallas kernels for 0%

profile of v1, /device:TPU:32, one launch (start us, length us, event | category | flops | bytes accessed | tf_op | source)
XLA Modules:
  0.0 178.9 jit_solution(14271580091972446832)
XLA Ops:
  0.6 0.0 copy-start.5
  0.6 0.0 copy-start
  0.7 0.7 copy.9
  1.4 32.9 %all_to_all.30 = bf16[16,16,4,128]{3,1,2,0:T(8,128)(2,1)S(1)} all-to-all(bf16[16,16,4,128]{3,1,2,0:T(8,128)(2,1)S(1)} %broadcast_in_dim.13), channel_id=1, replica_groups=mesh['z'=16,'c'=2,'tgt'=16] {'z'}, dimensions={0} | all-to-all | bytes 524288 | tf_op jit(solution)/shard_map/all_to_all | solution.py:231
  34.4 1.6 broadcast_in_dim.12
  36.0 7.0 %all-to-all-start = ((bf16[16,16,8,128]{3,2,1,0:T(8,128)(2,1)}), bf16[16,16,8,128]{3,2,1,0:T(8,128)(2,1)S(1)}, u32[]{:S(2)}, u32[]{:S(2)}) async-start(bf16[16,16,8,128]{3,2,1,0:T(8,128)(2,1)} %broadcast_in_dim.12), calls=%async_computation | async-start | bytes 1048576 | tf_op jit(solution)/shard_map/all_to_all | solution.py:231
  43.7 2.2 %all-gather = bf16[32,16,4,128]{3,1,2,0:T(8,128)(2,1)S(1)} all-gather(bf16[16,16,4,128]{3,1,2,0:T(8,128)(2,1)S(1)} %all_to_all.30), channel_id=2, replica_groups=mesh['z'=16,'c'=2,'tgt'=16] {'c'}, dimensions={0}, use_global_device_ids=true | all-gather | bytes 786432 | tf_op jit(solution)/shard_map/all_gather | solution.py:245
  45.9 0.2 copy.10
  46.1 7.7 %all-to-all-done.source = bf16[16,16,8,128]{3,2,1,0:T(8,128)(2,1)S(1)} async-done(((bf16[16,16,8,128]{3,2,1,0:T(8,128)(2,1)}), bf16[16,16,8,128]{3,2,1,0:T(8,128)(2,1)S(1)}, u32[]{:S(2)}, u32[]{:S(2)}) %all-to-all-start) | async-done | bytes 524320 | tf_op jit(solution)/shard_map/all_to_all | solution.py:231
  53.8 0.0 copy-start.3
  53.8 0.7 copy-done.3
  54.5 0.0 copy-start.6
  54.5 0.7 copy-done.6
  55.2 2.3 %shard_map.86 = (f32[128,128,128]{2,1,0:T(8,128)S(1)}, bf16[16,128,128]{2,1,0:T(8,128)(2,1)S(1)}, bf16[16,128,128]{2,1,0:T(8,128)(2,1)S(1)}, f32[16,16,128]{2,1,0:T(8,128)S(1)}) custom-call(s32[1]{0:T(128)} %bitcast.91.count_ref, s32[2,128]{1,0:T(2,128)S(1)} %bitcast.96, bf16[16,16,8,128]{3,2,1,0:T(8,128)(2,1)S(1)} %all-to-all-done.source, ...), custom_call_target="tpu_custom_call" | custom-call | tf_op jit(solution)/shard_map/pallas_call | solution.py:216
  57.5 15.2 %all_to_all.31.gathered = f32[16,16,128]{2,1,0:T(8,128)S(1)} all-to-all(f32[16,16,128]{2,1,0:T(8,128)S(1)} %get-tuple-element.12), channel_id=1, replica_groups=mesh['z'=16,'c'=2,'tgt'=16] {'tgt'}, dimensions={0} | all-to-all | bytes 262144 | tf_op jit(solution)/shard_map/all_to_all | solution.py:231
  72.7 0.0 copy-start.1
  72.7 0.7 copy-done.1
  73.4 0.0 copy-start.4
  73.4 0.7 copy-done.4
  74.1 0.0 copy-start.2
  74.1 5.1 %shard_map.87 = (f32[16,128]{1,0:T(8,128)}, f32[16,128]{1,0:T(8,128)S(1)}) custom-call(s32[1]{0:T(128)} %bitcast.92.count_ref, s32[2,128]{1,0:T(2,128)S(1)} %bitcast.97, f32[128,128,128]{2,1,0:T(8,128)S(1)} %get-tuple-element.9.cached, bf16[16,128,128]{2,1,0:T(8,128)(2,1)S(1)} %get-tuple-element.10.rows, ...), custom_call_target="tpu_custom_call" | custom-call | tf_op jit(solution)/shard_map/pallas_call | solution.py:216
  79.2 1.8 %all-gather.1 = f32[32,128]{1,0:T(8,128)S(1)} all-gather(f32[16,128]{1,0:T(8,128)S(1)} %get-tuple-element.13), channel_id=3, replica_groups=mesh['z'=16,'c'=2,'tgt'=16] {'c'}, dimensions={0}, use_global_device_ids=true | all-gather | bytes 24576 | tf_op jit(solution)/shard_map/all_gather | solution.py:276
  81.0 39.7 %all_to_all.32.gathered = f32[16,16,128]{2,1,0:T(8,128)S(1)} all-to-all(f32[16,16,128]{2,1,0:T(8,128)S(1)} %broadcast_in_dim.15), channel_id=1, replica_groups=mesh['z'=16,'c'=2,'tgt'=16] {'z'}, dimensions={0} | all-to-all | bytes 262144 | tf_op jit(solution)/shard_map/all_to_all | solution.py:231
  120.7 0.0 copy-done.5
  120.7 0.0 copy-done
  120.8 1.3 shard_map.88
  122.0 12.6 %all_to_all.33.gathered = f32[16,16,128]{2,1,0:T(8,128)S(1)} all-to-all(f32[16,16,128]{2,1,0:T(8,128)S(1)} %shard_map.88), channel_id=1, replica_groups=mesh['z'=16,'c'=2,'tgt'=16] {'tgt'}, dimensions={0} | all-to-all | bytes 262144 | tf_op jit(solution)/shard_map/all_to_all | solution.py:231
  134.6 0.0 copy-done.2
  134.6 5.1 %shard_map.89 = (f32[16,128]{1,0:T(8,128)}, f32[16,128]{1,0:T(8,128)S(1)}) custom-call(s32[1]{0:T(128)} %bitcast.94.count_ref, s32[2,128]{1,0:T(2,128)S(1)} %bitcast.99, f32[128,128,128]{2,1,0:T(8,128)S(1)} %get-tuple-element.9.cached, bf16[16,128,128]{2,1,0:T(8,128)(2,1)S(1)} %get-tuple-element.10.rows, ...), custom_call_target="tpu_custom_call" | custom-call | tf_op jit(solution)/shard_map/pallas_call | solution.py:216
  139.7 1.8 %all-gather.2 = f32[32,128]{1,0:T(8,128)S(1)} all-gather(f32[16,128]{1,0:T(8,128)S(1)} %get-tuple-element.15), channel_id=4, replica_groups=mesh['z'=16,'c'=2,'tgt'=16] {'c'}, dimensions={0}, use_global_device_ids=true | all-gather | bytes 24576 | tf_op jit(solution)/shard_map/all_gather | solution.py:276
  141.5 36.8 %all_to_all.34 = f32[16,16,128]{2,1,0:T(8,128)S(1)} all-to-all(f32[16,16,128]{2,1,0:T(8,128)S(1)} %broadcast_in_dim.33), channel_id=1, replica_groups=mesh['z'=16,'c'=2,'tgt'=16] {'z'}, dimensions={0} | all-to-all | bytes 262144 | tf_op jit(solution)/shard_map/all_to_all | solution.py:231
  178.3 0.7 add_subtract_fusion
  (5 shorter events, 0.1 us)
Async XLA Ops:
  0.6 120.1 %copy-start.5 = (s32[1,1,128,2]{2,3,1,0:T(2,128)S(1)}, s32[1,1,128,2]{2,3,1,0:T(2,128)}, u32[]{:S(2)}) copy-start(s32[1,1,128,2]{2,3,1,0:T(2,128)} %param.12) | copy-start | bytes 3076
  0.6 120.1 %copy-start = (f32[16,128]{1,0:T(8,128)S(1)}, f32[16,128]{1,0:T(8,128)}, u32[]{:S(2)}) copy-start(f32[16,128]{1,0:T(8,128)} %mass.4) | copy-start | bytes 24580
  36.0 17.8 %all-to-all-start = ((bf16[16,16,8,128]{3,2,1,0:T(8,128)(2,1)}), bf16[16,16,8,128]{3,2,1,0:T(8,128)(2,1)S(1)}, u32[]{:S(2)}, u32[]{:S(2)}) async-start(bf16[16,16,8,128]{3,2,1,0:T(8,128)(2,1)} %broadcast_in_dim.12), calls=%async_computation | async-start | bytes 1048576 | tf_op jit(solution)/shard_map/all_to_all | solution.py:231
  53.8 0.7 copy-start.3
  54.5 0.7 copy-start.6
  72.7 0.7 copy-start.1
  73.4 0.7 copy-start.4
  74.1 60.5 %copy-start.2 = (f32[16,128]{1,0:T(8,128)S(1)}, f32[16,128]{1,0:T(8,128)}, u32[]{:S(2)}) copy-start(f32[16,128]{1,0:T(8,128)} %mass.5) | copy-start | bytes 24580

commit v2 on v1

--- a/solution.py
+++ b/solution.py
@@ -241,7 +241,7 @@
     source_blocks, frames, _ = source_embed.shape
     target_blocks = target_embed.shape[0]
     columns_gathered = exchanged(copies(jnp.swapaxes(target_embed, 1, 2), "z"), "z")
-    source = exchanged(copies(jnp.swapaxes(source_embed, 1, 2), "tgt"), "tgt")
+    source = lax.all_gather(jnp.swapaxes(source_embed, 1, 2), "tgt")
     target = lax.all_gather(columns_gathered, "c")
     across = lax.axis_size("tgt")
     features = across * source_embed.shape[2]

time: 180 us -> 175 us (0.972)
  the two profiles are of different devices: /device:TPU:32 before, /device:TPU:6 now
where the time goes in v2:
time: 175 us
  blocking collectives  121 us (69%)
  Pallas kernels  33.1 us (19%)
  starting transfers between devices  15.2 us (9%)
  local copies, waits for them, and re-layouts  3.83 us (2%)
    all_to_all x4, blocking collectives, exchanged(): return lax.all_to_all(x, axis, 0, 0, tiled=True)  90.9 us
    pallas_call x4, Pallas kernels, called(): pl.pallas_call(body, out_shape=outs, in_specs=[smem, smem] + [vmem] * (le...  33.1 us
    all_gather x1, blocking collectives, on_device(): source = lax.all_gather(jnp.swapaxes(source_embed, 1, 2), 'tgt')  23.9 us
    all_to_all x1, starting transfers between devices, exchanged(): return lax.all_to_all(x, axis, 0, 0, tiled=True)  15.2 us
    all_gather x2, blocking collectives, on_device(): both = lax.all_gather(partial, 'c')  3.6 us
  transfers between devices with their start and end apart: 1, of which 0 were waited for; matrix products, arithmetic and copies ran while one was open for 0% of the time, Pallas kernels for 0%

profile of v2, /device:TPU:6, one launch (start us, length us, event | category | flops | bytes accessed | tf_op | source)
XLA Modules:
  0.0 174.8 jit_solution(8442702834387610787)
XLA Ops:
  0.6 0.0 copy-start
  0.6 0.7 copy.9
  1.4 0.8 broadcast_in_dim.10
  2.1 15.2 %all-to-all-start = ((bf16[16,16,4,128]{3,1,2,0:T(8,128)(2,1)}), bf16[16,16,4,128]{3,1,2,0:T(8,128)(2,1)S(1)}, u32[]{:S(2)}, u32[]{:S(2)}) async-start(bf16[16,16,4,128]{3,1,2,0:T(8,128)(2,1)} %broadcast_in_dim.10), calls=%async_computation | async-start | bytes 524288 | tf_op jit(solution)/shard_map/all_to_all | solution.py:231
  18.0 23.9 %all-gather = bf16[256,8,128]{2,1,0:T(8,128)(2,1)S(1)} all-gather(bf16[16,8,128]{2,1,0:T(8,128)(2,1)} %bitcast.102), channel_id=2, replica_groups=mesh['z'=16,'c'=2,'tgt'=16] {'tgt'}, dimensions={0}, use_global_device_ids=true | all-gather | bytes 557056 | tf_op jit(solution)/shard_map/all_gather | solution.py:244
  41.9 0.0 all-to-all-done
  41.9 2.2 %all-gather.1 = bf16[32,16,4,128]{3,1,2,0:T(8,128)(2,1)S(1)} all-gather(bf16[16,16,4,128]{3,1,2,0:T(8,128)(2,1)S(1)} %all-to-all-done), channel_id=3, replica_groups=mesh['z'=16,'c'=2,'tgt'=16] {'c'}, dimensions={0}, use_global_device_ids=true | all-gather | bytes 786432 | tf_op jit(solution)/shard_map/all_gather | solution.py:245
  44.1 0.2 copy.10
  44.3 0.0 copy-start.3
  44.3 0.7 copy-done.3
  45.0 0.0 copy-start.4
  45.0 0.7 copy-done.4
  45.7 4.9 %shard_map.86 = (f32[128,128,128]{2,1,0:T(8,128)S(1)}, bf16[16,128,128]{2,1,0:T(8,128)(2,1)S(1)}, bf16[16,128,128]{2,1,0:T(8,128)(2,1)S(1)}, f32[16,16,128]{2,1,0:T(8,128)S(1)}) custom-call(s32[1]{0:T(128)} %bitcast.92.count_ref, s32[2,128]{1,0:T(2,128)S(1)} %bitcast.98, bf16[16,16,8,128]{3,2,1,0:T(8,128)(2,1)S(1)} %bitcast.96, ...), custom_call_target="tpu_custom_call" | custom-call | tf_op jit(solution)/shard_map/pallas_call | solution.py:216
  50.6 13.2 %all_to_all.25.gathered = f32[16,16,128]{2,1,0:T(8,128)S(1)} all-to-all(f32[16,16,128]{2,1,0:T(8,128)S(1)} %get-tuple-element.12), channel_id=1, replica_groups=mesh['z'=16,'c'=2,'tgt'=16] {'tgt'}, dimensions={0} | all-to-all | bytes 262144 | tf_op jit(solution)/shard_map/all_to_all | solution.py:231
  63.8 0.0 copy-start.1
  63.8 0.7 copy-done.1
  64.5 0.0 copy-start.2
  64.5 13.3 %shard_map.87 = (f32[16,128]{1,0:T(8,128)}, f32[16,128]{1,0:T(8,128)S(1)}) custom-call(s32[1]{0:T(128)} %bitcast.93.count_ref, s32[2,128]{1,0:T(2,128)S(1)} %bitcast.99, f32[128,128,128]{2,1,0:T(8,128)S(1)} %get-tuple-element.9.cached, bf16[16,128,128]{2,1,0:T(8,128)(2,1)S(1)} %get-tuple-element.10.rows, ...), custom_call_target="tpu_custom_call" | custom-call | tf_op jit(solution)/shard_map/pallas_call | solution.py:216
  77.8 1.8 %all-gather.2 = f32[32,128]{1,0:T(8,128)S(1)} all-gather(f32[16,128]{1,0:T(8,128)S(1)} %get-tuple-element.13), channel_id=4, replica_groups=mesh['z'=16,'c'=2,'tgt'=16] {'c'}, dimensions={0}, use_global_device_ids=true | all-gather | bytes 24576 | tf_op jit(solution)/shard_map/all_gather | solution.py:276
  79.6 30.8 %all_to_all.26.gathered = f32[16,16,128]{2,1,0:T(8,128)S(1)} all-to-all(f32[16,16,128]{2,1,0:T(8,128)S(1)} %broadcast_in_dim.24), channel_id=1, replica_groups=mesh['z'=16,'c'=2,'tgt'=16] {'z'}, dimensions={0} | all-to-all | bytes 262144 | tf_op jit(solution)/shard_map/all_to_all | solution.py:231
  110.4 0.0 copy-done
  110.4 1.7 shard_map.88
  112.1 17.4 %all_to_all.27.gathered = f32[16,16,128]{2,1,0:T(8,128)S(1)} all-to-all(f32[16,16,128]{2,1,0:T(8,128)S(1)} %shard_map.88), channel_id=1, replica_groups=mesh['z'=16,'c'=2,'tgt'=16] {'tgt'}, dimensions={0} | all-to-all | bytes 262144 | tf_op jit(solution)/shard_map/all_to_all | solution.py:231
  129.6 0.0 copy-done.2
  129.6 13.3 %shard_map.89 = (f32[16,128]{1,0:T(8,128)}, f32[16,128]{1,0:T(8,128)S(1)}) custom-call(s32[1]{0:T(128)} %bitcast.95.count_ref, s32[2,128]{1,0:T(2,128)S(1)} %bitcast.101, f32[128,128,128]{2,1,0:T(8,128)S(1)} %get-tuple-element.9.cached, bf16[16,128,128]{2,1,0:T(8,128)(2,1)S(1)} %get-tuple-element.10.rows, ...), custom_call_target="tpu_custom_call" | custom-call | tf_op jit(solution)/shard_map/pallas_call | solution.py:216
  142.8 1.8 %all-gather.3 = f32[32,128]{1,0:T(8,128)S(1)} all-gather(f32[16,128]{1,0:T(8,128)S(1)} %get-tuple-element.15), channel_id=5, replica_groups=mesh['z'=16,'c'=2,'tgt'=16] {'c'}, dimensions={0}, use_global_device_ids=true | all-gather | bytes 24576 | tf_op jit(solution)/shard_map/all_gather | solution.py:276
  144.7 29.4 %all_to_all.28 = f32[16,16,128]{2,1,0:T(8,128)S(1)} all-to-all(f32[16,16,128]{2,1,0:T(8,128)S(1)} %broadcast_in_dim.26), channel_id=1, replica_groups=mesh['z'=16,'c'=2,'tgt'=16] {'z'}, dimensions={0} | all-to-all | bytes 262144 | tf_op jit(solution)/shard_map/all_to_all | solution.py:231
  174.1 0.7 add_subtract_fusion
  (4 shorter events, 0.1 us)
Async XLA Ops:
  0.6 109.8 %copy-start = (f32[16,128]{1,0:T(8,128)S(1)}, f32[16,128]{1,0:T(8,128)}, u32[]{:S(2)}) copy-start(f32[16,128]{1,0:T(8,128)} %mass.4) | copy-start | bytes 24580
  2.1 39.8 %all-to-all-start = ((bf16[16,16,4,128]{3,1,2,0:T(8,128)(2,1)}), bf16[16,16,4,128]{3,1,2,0:T(8,128)(2,1)S(1)}, u32[]{:S(2)}, u32[]{:S(2)}) async-start(bf16[16,16,4,128]{3,1,2,0:T(8,128)(2,1)} %broadcast_in_dim.10), calls=%async_computation | async-start | bytes 524288 | tf_op jit(solution)/shard_map/all_to_all | solution.py:231
  44.3 0.7 copy-start.3
  45.0 0.7 copy-start.4
  63.8 0.7 copy-start.1
  64.5 65.1 %copy-start.2 = (f32[16,128]{1,0:T(8,128)S(1)}, f32[16,128]{1,0:T(8,128)}, u32[]{:S(2)}) copy-start(f32[16,128]{1,0:T(8,128)} %mass.5) | copy-start | bytes 24580

commit v3 on v2

--- a/solution.py
+++ b/solution.py
@@ -16,7 +16,8 @@
 empty_peak = -1e30
 log2e = 1.0 / math.log(2.0)
 to_log2 = log2e / smoothing_epsilon
-group = 4
+group = 16
+light_group = 8
 pot_most = 20.0
 sum_least = 4.3e-18
 sum_most = 5e34
@@ -34,17 +35,23 @@
     )
 
 
-def over_slots(count, body):
-    whole = count // group
+def over_slots(count, size, body):
+    whole = count // size
 
     @pl.loop(0, whole)
     def _(step):
-        for lane in range(group):
-            body(step * group + lane)
-
-    @pl.loop(whole * group, count)
-    def _(slot):
-        body(slot)
+        for lane in range(size):
+            body(step * size + lane, None)
+
+    @pl.when(whole * size < count)
+    def _():
+        for lane in range(size):
+            slot = whole * size + lane
+            body(slot, slot < count)
+
+
+def kept_only(value, live):
+    return value if live is None else jnp.where(live, value, 0.0)
 
 
 def within(potential, sums):
@@ -112,17 +119,16 @@
     partial[...] = jnp.broadcast_to(sums[...][None], partial.shape)
 
 
-def row_pass(count, pairs, rows, columns, potential, kernel_of, weights, total, peak, sums, partial):
+def row_pass(size, count, pairs, rows, columns, potential, kernel_of, weights, total, peak, sums, partial):
     weights[...] = jnp.exp(potential[...])
     total[...] = jnp.zeros_like(total)
 
-    def body(slot):
+    def body(slot, live):
         source, target = pairs[0, slot], pairs[1, slot]
-        total[source] = total[source] + kernel_of(slot, source, target) * weights[
-            pl.ds(target, 1), :
-        ]
-
-    over_slots(count, body)
+        value = kernel_of(slot, source, target) * weights[pl.ds(target, 1), :]
+        total[source] = total[source] + kept_only(value, live)
+
+    over_slots(count, size, body)
     rows_kept(sums, lambda block: jnp.sum(total[block].T, axis=0, keepdims=True))
     fine = within(potential[...], sums[...])
 
@@ -138,9 +144,15 @@
 
 
 def first_kernel(
-    count_ref, pairs, source, target, start, cached, rows, columns, partial,
-    wide_source, wide_target, weights, total, peak, sums,
+    count_ref, far_pairs, far_start, far_source_mass, far_target_mass, source, target,
+    cached, rows, columns, near_pairs, source_mass, target_mass, partial,
+    pairs, start, arrived, wide_source, wide_target, weights, total, peak, sums,
 ):
+    moves = fetches(
+        (far_pairs, far_start, far_pairs, far_source_mass, far_target_mass),
+        (pairs, start, near_pairs, source_mass, target_mass),
+        arrived,
+    )
     blocks = source.shape[1]
     features = source.shape[2]
     for device in range(source.shape[0]):
@@ -156,34 +168,43 @@
         rows[block] = wide_source[block].T.astype(jnp.bfloat16)
         columns[block] = wide_target[block].astype(jnp.bfloat16)
 
+    for move in moves[:2]:
+        move.wait()
+
     def kernel_of(slot, source, target):
         value = jnp.exp2(scores(rows[source], columns[target]) * to_log2)
         cached[slot] = value
         return value
 
     row_pass(
-        count_ref[0], pairs, rows, columns, start, kernel_of, weights, total, peak, sums, partial
-    )
+        group, count_ref[0], pairs, rows, columns, start, kernel_of, weights, total, peak, sums, partial
+    )
+    for move in moves[2:]:
+        move.wait()
 
 
 def column_kernel(
-    count_ref, pairs, cached, rows, columns, gathered, mass, scaling, partial,
-    wide, slim, total, peak, sums,
+    count_ref, near_pairs, mass, cached, rows, columns, gathered, scaling, partial,
+    pairs, arrived, wide, slim, total, peak, sums,
 ):
+    moves = fetches((near_pairs,), (pairs,), arrived)
     count = count_ref[0]
-    scaling[...] = mass[...] - log_sum_exp([gathered[k] for k in range(gathered.shape[0])])
+    reached = log_sum_exp([gathered[k] for k in range(gathered.shape[0])])
+    for move in moves:
+        move.wait()
+    scaling[...] = mass[...] - reached
     weights = jnp.exp(scaling[...])
     for block in range(wide.shape[0]):
         wide[block] = jnp.broadcast_to(weights[block : block + 1, :], wide.shape[1:]).T
     slim[...] = jnp.zeros_like(slim)
 
-    def body(slot):
+    def body(slot, live):
         source, target = pairs[0, slot], pairs[1, slot]
         value = cached[slot] * wide[source]
-        value = value.reshape(-1, 8, value.shape[-1])
-        slim[target] = slim[target] + jnp.sum(value, axis=0)
-
-    over_slots(count, body)
+        value = jnp.sum(value.reshape(-1, 8, value.shape[-1]), axis=0)
+        slim[target] = slim[target] + kept_only(value, live)
+
+    over_slots(count, light_group, body)
     rows_kept(sums, lambda block: jnp.sum(slim[block], axis=0, keepdims=True))
     fine = within(scaling[...], sums[...])
 
@@ -199,28 +220,46 @@
 
 
 def row_kernel(
-    count_ref, pairs, cached, rows, columns, gathered, mass, partial,
-    potential, weights, total, peak, sums,
+    count_ref, near_pairs, mass, cached, rows, columns, gathered, partial,
+    pairs, arrived, potential, weights, total, peak, sums,
 ):
-    potential[...] = mass[...] - log_sum_exp([gathered[k] for k in range(gathered.shape[0])])
+    moves = fetches((near_pairs,), (pairs,), arrived)
+    reached = log_sum_exp([gathered[k] for k in range(gathered.shape[0])])
+    for move in moves:
+        move.wait()
+    potential[...] = mass[...] - reached
     row_pass(
-        count_ref[0], pairs, rows, columns, potential,
+        light_group, count_ref[0], pairs, rows, columns, potential,
         lambda slot, source, target: cached[slot],
         weights, total, peak, sums, partial,
     )
 
 
-def called(body, outs, scratch, *operands):
+def called(body, outs, scratch, *operands, far=0):
     smem = pl.BlockSpec(memory_space=pltpu.SMEM)
     vmem = pl.BlockSpec(memory_space=pltpu.VMEM)
+    anywhere = pl.BlockSpec(memory_space=pl.ANY)
+    count, *rest = operands
+    spaces = [pltpu.HBM] * far + [pltpu.VMEM] * (len(rest) - far)
+    held = [pltpu.with_memory_space_constraint(x, space) for x, space in zip(rest, spaces)]
     return pl.pallas_call(
         body,
         out_shape=outs,
-        in_specs=[smem, smem] + [vmem] * (len(operands) - 2),
+        in_specs=[smem] + [anywhere] * far + [vmem] * (len(rest) - far),
         out_specs=[vmem] * len(outs),
         scratch_shapes=scratch,
         compiler_params=pltpu.CompilerParams(vmem_limit_bytes=40 * 1024 * 1024),
-    )(*operands)
+    )(count, *held)
+
+
+def fetches(sources, places, arrived):
+    moves = [
+        pltpu.make_async_copy(source, place, arrived.at[k])
+        for k, (source, place) in enumerate(zip(sources, places))
+    ]
+    for move in moves:
+        move.start()
+    return moves
 
 
 def copies(x, axis):
@@ -231,60 +270,74 @@
     return lax.all_to_all(x, axis, 0, 0, tiled=True)
 
 
-def on_device(
-    source_embed, target_embed, source_mass, target_mass, target_start, block_pairs, counts
-):
+def local_chain(source, target, start, source_mass, target_mass, pairs, count, over_tgt, over_src):
     f32, bf16 = jnp.float32, jnp.bfloat16
-    slots = block_pairs.shape[2]
-    pairs = block_pairs.reshape(slots, 2).T
-    count = counts.reshape(1)
-    source_blocks, frames, _ = source_embed.shape
-    target_blocks = target_embed.shape[0]
-    columns_gathered = exchanged(copies(jnp.swapaxes(target_embed, 1, 2), "z"), "z")
-    source = lax.all_gather(jnp.swapaxes(source_embed, 1, 2), "tgt")
-    target = lax.all_gather(columns_gathered, "c")
-    across = lax.axis_size("tgt")
-    features = across * source_embed.shape[2]
+    slots = pairs.shape[1]
+    across, source_blocks, depth, frames = source.shape
+    target_blocks = target.shape[2]
+    features = across * depth
     line = jax.ShapeDtypeStruct((source_blocks, frames), f32)
     many = jax.ShapeDtypeStruct((across, source_blocks, frames), f32)
     square = pltpu.VMEM((source_blocks, frames, frames), f32)
     flat = pltpu.VMEM((source_blocks, frames), f32)
-    cached, rows, columns, partial = called(
+    copied = pltpu.VMEM(pairs.shape, jnp.int32)
+    listed = pltpu.SMEM(pairs.shape, jnp.int32)
+    arrivals = pltpu.SemaphoreType.DMA
+    *kept, near_pairs, source_mass, target_mass, partial = called(
         first_kernel,
         [
             pltpu.VMEM((slots, frames, frames), f32),
             pltpu.VMEM((source_blocks, frames, features), bf16),
             pltpu.VMEM((target_blocks, features, frames), bf16),
-            many,
+            copied, flat, flat, many,
         ],
         [
+            listed, flat, arrivals((5,)),
             pltpu.VMEM((source_blocks, features, frames), f32),
             pltpu.VMEM((target_blocks, features, frames), f32),
             flat, square, square, flat,
         ],
-        count, pairs, source, target, target_start,
-    )
-    kept = [count, pairs]
-    kept += [pltpu.with_memory_space_constraint(x, pltpu.VMEM) for x in (cached, rows, columns)]
+        count, pairs, start, source_mass, target_mass, source, target,
+        far=4,
+    )
     for iteration in range(ITERS):
         scaling, partial = called(
             column_kernel,
             [line, line],
-            [square, pltpu.VMEM((target_blocks, 8, frames), f32), square, square, flat],
-            *kept, exchanged(partial, "tgt"), source_mass,
+            [
+                listed, arrivals((1,)), square,
+                pltpu.VMEM((target_blocks, 8, frames), f32), square, square, flat,
+            ],
+            count, near_pairs, source_mass, *kept, over_tgt(partial),
         )
-        both = lax.all_gather(partial, "c")
-        merged = log_sum_exp([both[0], both[1]])
-        gathered = exchanged(copies(merged, "z"), "z")
+        gathered = over_src(partial)
         if iteration < ITERS - 1:
             (partial,) = called(
                 row_kernel,
                 [many],
-                [flat, flat, square, square, flat],
-                *kept, gathered, target_mass,
+                [listed, arrivals((1,)), flat, flat, square, square, flat],
+                count, near_pairs, target_mass, *kept, gathered,
             )
     potential = target_mass - log_sum_exp([gathered[k] for k in range(gathered.shape[0])])
     return scaling, potential
+
+
+def over_src(partial):
+    both = lax.all_gather(partial, "c")
+    return exchanged(copies(log_sum_exp([both[0], both[1]]), "z"), "z")
+
+
+def on_device(
+    source_embed, target_embed, source_mass, target_mass, target_start, block_pairs, counts
+):
+    pairs = block_pairs.reshape(block_pairs.shape[2], 2).T
+    columns = exchanged(copies(jnp.swapaxes(target_embed, 1, 2), "z"), "z")
+    return local_chain(
+        lax.all_gather(jnp.swapaxes(source_embed, 1, 2), "tgt"),
+        lax.all_gather(columns, "c"),
+        target_start, source_mass, target_mass, pairs, counts.reshape(1),
+        lambda partial: exchanged(partial, "tgt"), over_src,
+    )
 
 
 def solution(mesh):

time: 175 us -> 179 us (1.023)
  the two profiles are of different devices: /device:TPU:6 before, /device:TPU:28 now
where the time goes in v3:
time: 179 us; the launch traced here: 178 us
  blocking collectives  105 us (59%)
  Pallas kernels  54.6 us (31%)
  starting transfers between devices  15.2 us (8%)
    all_to_all x4, blocking collectives, exchanged(): return lax.all_to_all(x, axis, 0, 0, tiled=True)  76.9 us
    pallas_call x4, Pallas kernels, called(): pl.pallas_call(body, out_shape=outs, in_specs=[smem] + [anywhere] * far +...  54.6 us
    all_gather x1, blocking collectives, on_device(): lax.all_gather(jnp.swapaxes(source_embed, 1, 2), 'tgt')  22.1 us
    all_to_all x1, starting transfers between devices, exchanged(): return lax.all_to_all(x, axis, 0, 0, tiled=True)  15.2 us
    all_gather x2, blocking collectives, over_src(): both = lax.all_gather(partial, 'c')  3.63 us
  transfers between devices with their start and end apart: 1, of which 0 were waited for; matrix products, arithmetic and copies ran while one was open for 0% of the time, Pallas kernels for 0%

profile of v3, /device:TPU:28, one launch (start us, length us, event | category | flops | bytes accessed | tf_op | source)
XLA Modules:
  0.0 178.4 jit_solution(2365571534250149147)
XLA Ops:
  0.6 0.7 copy.9
  1.4 0.7 broadcast_in_dim.10
  2.1 15.2 %all-to-all-start = ((bf16[16,16,4,128]{3,1,2,0:T(8,128)(2,1)}), bf16[16,16,4,128]{3,1,2,0:T(8,128)(2,1)S(1)}, u32[]{:S(2)}, u32[]{:S(2)}) async-start(bf16[16,16,4,128]{3,1,2,0:T(8,128)(2,1)} %broadcast_in_dim.10), calls=%async_computation | async-start | bytes 524288 | tf_op jit(solution)/shard_map/all_to_all | solution.py:270
  17.9 22.1 %all-gather = bf16[256,8,128]{2,1,0:T(8,128)(2,1)S(1)} all-gather(bf16[16,8,128]{2,1,0:T(8,128)(2,1)} %bitcast.98), channel_id=2, replica_groups=mesh['z'=16,'c'=2,'tgt'=16] {'tgt'}, dimensions={0}, use_global_device_ids=true | all-gather | bytes 557056 | tf_op jit(solution)/shard_map/all_gather | solution.py:336
  40.0 0.0 all-to-all-done
  40.1 2.2 %all-gather.1 = bf16[32,16,4,128]{3,1,2,0:T(8,128)(2,1)S(1)} all-gather(bf16[16,16,4,128]{3,1,2,0:T(8,128)(2,1)S(1)} %all-to-all-done), channel_id=3, replica_groups=mesh['z'=16,'c'=2,'tgt'=16] {'c'}, dimensions={0}, use_global_device_ids=true | all-gather | bytes 786432 | tf_op jit(solution)/shard_map/all_gather | solution.py:337
  42.2 0.2 copy.10
  42.5 4.1 %shard_map.86 = (f32[128,128,128]{2,1,0:T(8,128)S(1)}, bf16[16,128,128]{2,1,0:T(8,128)(2,1)S(1)}, bf16[16,128,128]{2,1,0:T(8,128)(2,1)S(1)}, s32[2,128]{1,0:T(2,...) custom-call(s32[1]{0:T(128)} %bitcast.92.count_ref, s32[2,128]{1,0:T(2,128)} %bitcast.100, ...), custom_call_target="tpu_custom_call" | custom-call | tf_op jit(solution)/shard_map/pallas_call | solution.py:245
  46.6 11.0 %all_to_all.25.gathered = f32[16,16,128]{2,1,0:T(8,128)S(1)} all-to-all(f32[16,16,128]{2,1,0:T(8,128)S(1)} %get-tuple-element.18), channel_id=1, replica_groups=mesh['z'=16,'c'=2,'tgt'=16] {'tgt'}, dimensions={0} | all-to-all | bytes 262144 | tf_op jit(solution)/shard_map/all_to_all | solution.py:270
  57.6 24.1 %shard_map.87 = (f32[16,128]{1,0:T(8,128)}, f32[16,128]{1,0:T(8,128)S(1)}) custom-call(s32[1]{0:T(128)} %bitcast.93.count_ref, s32[2,128]{1,0:T(2,128)S(1)} %get-tuple-element.12.near_pairs, f32[16,128]{1,0:T(8,128)S(1)} %get-tuple-element.13.mass, f32[128,128,128]{2,1,0:T(8,128)S(1)} %get-tuple-element.14.cached, ...), custom_call_target="tpu_custom_call" | custom-call | tf_op jit(solution)/shard_map/pallas_call | solution.py:245
  81.7 1.8 %all-gather.2 = f32[32,128]{1,0:T(8,128)S(1)} all-gather(f32[16,128]{1,0:T(8,128)S(1)} %get-tuple-element.19), channel_id=4, replica_groups=mesh['z'=16,'c'=2,'tgt'=16] {'c'}, dimensions={0}, use_global_device_ids=true | all-gather | bytes 24576 | tf_op jit(solution)/shard_map/all_gather | solution.py:326
  83.5 29.2 %all_to_all.26.gathered = f32[16,16,128]{2,1,0:T(8,128)S(1)} all-to-all(f32[16,16,128]{2,1,0:T(8,128)S(1)} %broadcast_in_dim.24), channel_id=1, replica_groups=mesh['z'=16,'c'=2,'tgt'=16] {'z'}, dimensions={0} | all-to-all | bytes 262144 | tf_op jit(solution)/shard_map/all_to_all | solution.py:270
  112.8 2.3 %shard_map.88 = f32[16,16,128]{2,1,0:T(8,128)S(1)} custom-call(s32[1]{0:T(128)} %bitcast.94.count_ref, s32[2,128]{1,0:T(2,128)S(1)} %get-tuple-element.12.near_pairs, f32[16,128]{1,0:T(8,128)S(1)} %get-tuple-element.17.mass, f32[128,128,128]{2,1,0:T(8,128)S(1)} %get-tuple-element.14.cached, bf16[16,128,128]{2,1,0:T(8,128)(2,1)S(1)} %get-tuple-element.15.rows, ...), custom_call_target="tpu_custom_call" | custom-call | tf_op jit(solution)/shard_map/pallas_call | solution.py:245
  115.1 11.0 %all_to_all.27.gathered = f32[16,16,128]{2,1,0:T(8,128)S(1)} all-to-all(f32[16,16,128]{2,1,0:T(8,128)S(1)} %shard_map.88), channel_id=1, replica_groups=mesh['z'=16,'c'=2,'tgt'=16] {'tgt'}, dimensions={0} | all-to-all | bytes 262144 | tf_op jit(solution)/shard_map/all_to_all | solution.py:270
  126.0 24.1 %shard_map.89 = (f32[16,128]{1,0:T(8,128)}, f32[16,128]{1,0:T(8,128)S(1)}) custom-call(s32[1]{0:T(128)} %bitcast.95.count_ref, s32[2,128]{1,0:T(2,128)S(1)} %get-tuple-element.12.near_pairs, f32[16,128]{1,0:T(8,128)S(1)} %get-tuple-element.13.mass, f32[128,128,128]{2,1,0:T(8,128)S(1)} %get-tuple-element.14.cached, ...), custom_call_target="tpu_custom_call" | custom-call | tf_op jit(solution)/shard_map/pallas_call | solution.py:245
  150.1 1.8 %all-gather.3 = f32[32,128]{1,0:T(8,128)S(1)} all-gather(f32[16,128]{1,0:T(8,128)S(1)} %get-tuple-element.21), channel_id=5, replica_groups=mesh['z'=16,'c'=2,'tgt'=16] {'c'}, dimensions={0}, use_global_device_ids=true | all-gather | bytes 24576 | tf_op jit(solution)/shard_map/all_gather | solution.py:326
  152.0 25.7 %all_to_all.28 = f32[16,16,128]{2,1,0:T(8,128)S(1)} all-to-all(f32[16,16,128]{2,1,0:T(8,128)S(1)} %broadcast_in_dim.26), channel_id=1, replica_groups=mesh['z'=16,'c'=2,'tgt'=16] {'z'}, dimensions={0} | all-to-all | bytes 262144 | tf_op jit(solution)/shard_map/all_to_all | solution.py:270
  177.7 0.7 add_subtract_fusion
  (4 shorter events, 0.1 us)
Async XLA Ops:
  2.1 38.0 %all-to-all-start = ((bf16[16,16,4,128]{3,1,2,0:T(8,128)(2,1)}), bf16[16,16,4,128]{3,1,2,0:T(8,128)(2,1)S(1)}, u32[]{:S(2)}, u32[]{:S(2)}) async-start(bf16[16,16,4,128]{3,1,2,0:T(8,128)(2,1)} %broadcast_in_dim.10), calls=%async_computation | async-start | bytes 524288 | tf_op jit(solution)/shard_map/all_to_all | solution.py:270

commit v4 on v3

--- a/solution.py
+++ b/solution.py
@@ -11,6 +11,7 @@
 
 ITERS = 2
 SRC = ("z", "c")
+TGT = ("y", "x")
 
 smoothing_epsilon = 4.0
 empty_peak = -1e30
@@ -331,30 +332,32 @@
     source_embed, target_embed, source_mass, target_mass, target_start, block_pairs, counts
 ):
     pairs = block_pairs.reshape(block_pairs.shape[2], 2).T
+    source = exchanged(copies(jnp.swapaxes(source_embed, 1, 2), "x"), "x")
+    source = lax.all_gather(source, "y", tiled=True)
     columns = exchanged(copies(jnp.swapaxes(target_embed, 1, 2), "z"), "z")
     return local_chain(
-        lax.all_gather(jnp.swapaxes(source_embed, 1, 2), "tgt"),
+        source,
         lax.all_gather(columns, "c"),
         target_start, source_mass, target_mass, pairs, counts.reshape(1),
-        lambda partial: exchanged(partial, "tgt"), over_src,
+        lambda partial: exchanged(partial, TGT), over_src,
     )
 
 
 def solution(mesh):
-    split = Mesh(mesh.devices.reshape(16, 2, mesh.shape["tgt"]), ("z", "c", "tgt"))
+    split = Mesh(mesh.devices.reshape(16, 2, 4, 4), (*SRC, *TGT))
     placed = (
-        P(SRC, None, "tgt"),
-        P("tgt", None, SRC),
+        P(SRC, None, TGT),
+        P(TGT, None, SRC),
         P(SRC, None),
-        P("tgt", None),
-        P("tgt", None),
-        P(SRC, "tgt", None, None),
-        P(SRC, "tgt"),
+        P(TGT, None),
+        P(TGT, None),
+        P(SRC, TGT, None, None),
+        P(SRC, TGT),
     )
     return jax.shard_map(
         on_device,
         mesh=split,
         in_specs=placed,
-        out_specs=(P(SRC, None), P("tgt", None)),
+        out_specs=(P(SRC, None), P(TGT, None)),
         check_vma=False,
     )

time: 179 us -> 198 us (1.11)
  the two profiles are of different devices: /device:TPU:28 before, /device:TPU:34 now
where the time goes in v4:
time: 198 us
  blocking collectives  149 us (75%)
  starting transfers between devices  20 us (10%)
  Pallas kernels  16.6 us (8%)
  waiting for transfers between devices  7.05 us (4%)
  local copies, waits for them, and re-layouts  3.17 us (2%)
    all_to_all x4, blocking collectives, exchanged(): return lax.all_to_all(x, axis, 0, 0, tiled=True)  97 us
    all_gather x2, blocking collectives, over_src(): both = lax.all_gather(partial, 'c')  35.7 us
    all_to_all x2, starting transfers between devices, exchanged(): return lax.all_to_all(x, axis, 0, 0, tiled=True)  20 us
    pallas_call x4, Pallas kernels, called(): pl.pallas_call(body, out_shape=outs, in_specs=[smem] + [anywhere] * far +...  16.6 us
    all_gather x1, blocking collectives, on_device(): source = lax.all_gather(source, 'y', tiled=True)  13.8 us
    all_to_all x2, waiting for transfers between devices, exchanged(): return lax.all_to_all(x, axis, 0, 0, tiled=True)  7.05 us
  transfers between devices with their start and end apart: 2, of which 2 were waited for; matrix products, arithmetic and copies ran while one was open for 0% of the time, Pallas kernels for 0%

profile of v4, /device:TPU:34, one launch (start us, length us, event | category | flops | bytes accessed | tf_op | source)
XLA Modules:
  0.0 197.5 jit_solution(11671845465118537849)
XLA Ops:
  0.6 1.4 broadcast_in_dim.12
  2.1 4.8 %all-to-all-start = ((bf16[4,16,8,128]{3,2,1,0:T(8,128)(2,1)}), bf16[4,16,8,128]{3,2,1,0:T(8,128)(2,1)S(1)}, u32[]{:S(2)}, u32[]{:S(2)}) async-start(bf16[4,16,8,128]{3,2,1,0:T(8,128)(2,1)} %broadcast_in_dim.12), calls=%async_computation | async-start | bytes 262144 | tf_op jit(solution)/shard_map/all_to_all | solution.py:271
  6.9 0.7 copy.9
  7.6 3.8 %all-to-all-done = bf16[4,16,8,128]{3,2,1,0:T(8,128)(2,1)S(1)} async-done(((bf16[4,16,8,128]{3,2,1,0:T(8,128)(2,1)}), bf16[4,16,8,128]{3,2,1,0:T(8,128)(2,1)S(1)}, u32[]{:S(2)}, u32[]{:S(2)}) %all-to-all-start) | async-done | bytes 131104 | tf_op jit(solution)/shard_map/all_to_all | solution.py:271
  11.4 0.8 broadcast_in_dim.13
  12.2 15.2 %all-to-all-start.1 = ((bf16[16,16,4,128]{3,1,2,0:T(8,128)(2,1)}), bf16[16,16,4,128]{3,1,2,0:T(8,128)(2,1)S(1)}, u32[]{:S(2)}, u32[]{:S(2)}) async-start(bf16[16,16,4,128]{3,1,2,0:T(8,128)(2,1)} %broadcast_in_dim.13), calls=%async_computation.1 | async-start | bytes 524288 | tf_op jit(solution)/shard_map/all_to_all | solution.py:271
  28.0 13.8 %all_gather.21.source = bf16[16,16,8,128]{3,2,1,0:T(8,128)(2,1)S(1)} all-gather(bf16[4,16,8,128]{3,2,1,0:T(8,128)(2,1)S(1)} %all-to-all-done), channel_id=1, replica_groups=mesh['z'=16,'c'=2,'y'=4,'x'=4] {'y'}, dimensions={0}, use_global_device_ids=true | all-gather | bytes 655360 | tf_op jit(solution)/shard_map/all_gather | solution.py:336
  41.8 3.3 %all-to-all-done.1 = bf16[16,16,4,128]{3,1,2,0:T(8,128)(2,1)S(1)} async-done(((bf16[16,16,4,128]{3,1,2,0:T(8,128)(2,1)}), bf16[16,16,4,128]{3,1,2,0:T(8,128)(2,1)S(1)}, u32[]{:S(2)}, u32[]{:S(2)}) %all-to-all-start.1) | async-done | bytes 262176 | tf_op jit(solution)/shard_map/all_to_all | solution.py:271
  45.1 2.2 %all-gather = bf16[32,16,4,128]{3,1,2,0:T(8,128)(2,1)S(1)} all-gather(bf16[16,16,4,128]{3,1,2,0:T(8,128)(2,1)S(1)} %all-to-all-done.1), channel_id=2, replica_groups=mesh['z'=16,'c'=2,'y'=4,'x'=4] {'c'}, dimensions={0}, use_global_device_ids=true | all-gather | bytes 786432 | tf_op jit(solution)/shard_map/all_gather | solution.py:340
  47.3 0.2 copy.10
  47.5 2.0 %shard_map.86 = (f32[128,128,128]{2,1,0:T(8,128)S(1)}, bf16[16,128,128]{2,1,0:T(8,128)(2,1)S(1)}, bf16[16,128,128]{2,1,0:T(8,128)(2,1)S(1)}, s32[2,128]{1,0:T(2,...) custom-call(s32[1]{0:T(128)} %bitcast.91.count_ref, s32[2,128]{1,0:T(2,128)} %bitcast.98, ...), custom_call_target="tpu_custom_call" | custom-call | tf_op jit(solution)/shard_map/pallas_call | solution.py:246
  49.6 15.0 %all_to_all.30.gathered = f32[16,16,128]{2,1,0:T(8,128)S(1)} all-to-all(f32[16,16,128]{2,1,0:T(8,128)S(1)} %get-tuple-element.18), channel_id=1, replica_groups=mesh['z'=16,'c'=2,'y'=4,'x'=4] {'y','x'}, dimensions={0} | all-to-all | bytes 262144 | tf_op jit(solution)/shard_map/all_to_all | solution.py:271
  64.6 6.6 %shard_map.87 = (f32[16,128]{1,0:T(8,128)}, f32[16,128]{1,0:T(8,128)S(1)}) custom-call(s32[1]{0:T(128)} %bitcast.92.count_ref, s32[2,128]{1,0:T(2,128)S(1)} %get-tuple-element.12.near_pairs, f32[16,128]{1,0:T(8,128)S(1)} %get-tuple-element.13.mass, f32[128,128,128]{2,1,0:T(8,128)S(1)} %get-tuple-element.14.cached, ...), custom_call_target="tpu_custom_call" | custom-call | tf_op jit(solution)/shard_map/pallas_call | solution.py:246
  71.2 17.8 %all-gather.1 = f32[32,128]{1,0:T(8,128)S(1)} all-gather(f32[16,128]{1,0:T(8,128)S(1)} %get-tuple-element.19), channel_id=3, replica_groups=mesh['z'=16,'c'=2,'y'=4,'x'=4] {'c'}, dimensions={0}, use_global_device_ids=true | all-gather | bytes 24576 | tf_op jit(solution)/shard_map/all_gather | solution.py:327
  89.1 34.7 %all_to_all.31.gathered = f32[16,16,128]{2,1,0:T(8,128)S(1)} all-to-all(f32[16,16,128]{2,1,0:T(8,128)S(1)} %broadcast_in_dim.15), channel_id=1, replica_groups=mesh['z'=16,'c'=2,'y'=4,'x'=4] {'z'}, dimensions={0} | all-to-all | bytes 262144 | tf_op jit(solution)/shard_map/all_to_all | solution.py:271
  123.8 1.4 shard_map.88
  125.2 9.7 %all_to_all.32.gathered = f32[16,16,128]{2,1,0:T(8,128)S(1)} all-to-all(f32[16,16,128]{2,1,0:T(8,128)S(1)} %shard_map.88), channel_id=1, replica_groups=mesh['z'=16,'c'=2,'y'=4,'x'=4] {'y','x'}, dimensions={0} | all-to-all | bytes 262144 | tf_op jit(solution)/shard_map/all_to_all | solution.py:271
  134.9 6.6 %shard_map.89 = (f32[16,128]{1,0:T(8,128)}, f32[16,128]{1,0:T(8,128)S(1)}) custom-call(s32[1]{0:T(128)} %bitcast.94.count_ref, s32[2,128]{1,0:T(2,128)S(1)} %get-tuple-element.12.near_pairs, f32[16,128]{1,0:T(8,128)S(1)} %get-tuple-element.13.mass, f32[128,128,128]{2,1,0:T(8,128)S(1)} %get-tuple-element.14.cached, ...), custom_call_target="tpu_custom_call" | custom-call | tf_op jit(solution)/shard_map/pallas_call | solution.py:246
  141.5 17.8 %all-gather.2 = f32[32,128]{1,0:T(8,128)S(1)} all-gather(f32[16,128]{1,0:T(8,128)S(1)} %get-tuple-element.21), channel_id=4, replica_groups=mesh['z'=16,'c'=2,'y'=4,'x'=4] {'c'}, dimensions={0}, use_global_device_ids=true | all-gather | bytes 24576 | tf_op jit(solution)/shard_map/all_gather | solution.py:327
  159.4 37.5 %all_to_all.33 = f32[16,16,128]{2,1,0:T(8,128)S(1)} all-to-all(f32[16,16,128]{2,1,0:T(8,128)S(1)} %broadcast_in_dim.33), channel_id=1, replica_groups=mesh['z'=16,'c'=2,'y'=4,'x'=4] {'z'}, dimensions={0} | all-to-all | bytes 262144 | tf_op jit(solution)/shard_map/all_to_all | solution.py:271
  196.9 0.7 add_subtract_fusion
  (4 shorter events, 0.1 us)
Async XLA Ops:
  2.1 9.3 %all-to-all-start = ((bf16[4,16,8,128]{3,2,1,0:T(8,128)(2,1)}), bf16[4,16,8,128]{3,2,1,0:T(8,128)(2,1)S(1)}, u32[]{:S(2)}, u32[]{:S(2)}) async-start(bf16[4,16,8,128]{3,2,1,0:T(8,128)(2,1)} %broadcast_in_dim.12), calls=%async_computation | async-start | bytes 262144 | tf_op jit(solution)/shard_map/all_to_all | solution.py:271
  12.2 33.0 %all-to-all-start.1 = ((bf16[16,16,4,128]{3,1,2,0:T(8,128)(2,1)}), bf16[16,16,4,128]{3,1,2,0:T(8,128)(2,1)S(1)}, u32[]{:S(2)}, u32[]{:S(2)}) async-start(bf16[16,16,4,128]{3,1,2,0:T(8,128)(2,1)} %broadcast_in_dim.13), calls=%async_computation.1 | async-start | bytes 524288 | tf_op jit(solution)/shard_map/all_to_all | solution.py:271

commit v5 on v3

--- a/solution.py
+++ b/solution.py
@@ -145,12 +145,12 @@
 
 def first_kernel(
     count_ref, far_pairs, far_start, far_source_mass, far_target_mass, source, target,
-    cached, rows, columns, near_pairs, source_mass, target_mass, partial,
-    pairs, start, arrived, wide_source, wide_target, weights, total, peak, sums,
+    cached, rows, columns, pairs, source_mass, target_mass, partial,
+    start, arrived, wide_source, wide_target, weights, total, peak, sums,
 ):
     moves = fetches(
-        (far_pairs, far_start, far_pairs, far_source_mass, far_target_mass),
-        (pairs, start, near_pairs, source_mass, target_mass),
+        (far_pairs, far_start, far_source_mass, far_target_mass),
+        (pairs, start, source_mass, target_mass),
         arrived,
     )
     blocks = source.shape[1]
@@ -184,14 +184,11 @@
 
 
 def column_kernel(
-    count_ref, near_pairs, mass, cached, rows, columns, gathered, scaling, partial,
-    pairs, arrived, wide, slim, total, peak, sums,
+    count_ref, pairs, mass, cached, rows, columns, gathered, partial, scaling,
+    wide, slim, total, peak, sums,
 ):
-    moves = fetches((near_pairs,), (pairs,), arrived)
     count = count_ref[0]
     reached = log_sum_exp([gathered[k] for k in range(gathered.shape[0])])
-    for move in moves:
-        move.wait()
     scaling[...] = mass[...] - reached
     weights = jnp.exp(scaling[...])
     for block in range(wide.shape[0]):
@@ -220,13 +217,10 @@
 
 
 def row_kernel(
-    count_ref, near_pairs, mass, cached, rows, columns, gathered, partial,
-    pairs, arrived, potential, weights, total, peak, sums,
+    count_ref, pairs, mass, cached, rows, columns, gathered, partial,
+    potential, weights, total, peak, sums,
 ):
-    moves = fetches((near_pairs,), (pairs,), arrived)
     reached = log_sum_exp([gathered[k] for k in range(gathered.shape[0])])
-    for move in moves:
-        move.wait()
     potential[...] = mass[...] - reached
     row_pass(
         light_group, count_ref[0], pairs, rows, columns, potential,
@@ -236,17 +230,21 @@
 
 
 def called(body, outs, scratch, *operands, far=0):
-    smem = pl.BlockSpec(memory_space=pltpu.SMEM)
-    vmem = pl.BlockSpec(memory_space=pltpu.VMEM)
-    anywhere = pl.BlockSpec(memory_space=pl.ANY)
     count, *rest = operands
-    spaces = [pltpu.HBM] * far + [pltpu.VMEM] * (len(rest) - far)
-    held = [pltpu.with_memory_space_constraint(x, space) for x, space in zip(rest, spaces)]
+    places = [
+        pltpu.HBM if k < far else pltpu.SMEM if jnp.issubdtype(x.dtype, jnp.integer) else pltpu.VMEM
+        for k, x in enumerate(rest)
+    ]
+    held = [pltpu.with_memory_space_constraint(x, place) for x, place in zip(rest, places)]
+    given = [
+        pltpu.SMEM if jnp.issubdtype(x.dtype, jnp.integer) else pltpu.VMEM for x in outs
+    ]
     return pl.pallas_call(
         body,
         out_shape=outs,
-        in_specs=[smem] + [anywhere] * far + [vmem] * (len(rest) - far),
-        out_specs=[vmem] * len(outs),
+        in_specs=[pl.BlockSpec(memory_space=pltpu.SMEM)]
+        + [pl.BlockSpec(memory_space=pl.ANY if x is pltpu.HBM else x) for x in places],
+        out_specs=[pl.BlockSpec(memory_space=x) for x in given],
         scratch_shapes=scratch,
         compiler_params=pltpu.CompilerParams(vmem_limit_bytes=40 * 1024 * 1024),
     )(count, *held)
@@ -276,23 +274,21 @@
     across, source_blocks, depth, frames = source.shape
     target_blocks = target.shape[2]
     features = across * depth
-    line = jax.ShapeDtypeStruct((source_blocks, frames), f32)
     many = jax.ShapeDtypeStruct((across, source_blocks, frames), f32)
     square = pltpu.VMEM((source_blocks, frames, frames), f32)
     flat = pltpu.VMEM((source_blocks, frames), f32)
-    copied = pltpu.VMEM(pairs.shape, jnp.int32)
     listed = pltpu.SMEM(pairs.shape, jnp.int32)
     arrivals = pltpu.SemaphoreType.DMA
-    *kept, near_pairs, source_mass, target_mass, partial = called(
+    *kept, pairs, source_mass, target_mass, partial = called(
         first_kernel,
         [
             pltpu.VMEM((slots, frames, frames), f32),
             pltpu.VMEM((source_blocks, frames, features), bf16),
             pltpu.VMEM((target_blocks, features, frames), bf16),
-            copied, flat, flat, many,
+            listed, flat, flat, many,
         ],
         [
-            listed, flat, arrivals((5,)),
+            flat, arrivals((4,)),
             pltpu.VMEM((source_blocks, features, frames), f32),
             pltpu.VMEM((target_blocks, features, frames), f32),
             flat, square, square, flat,
@@ -301,22 +297,22 @@
         far=4,
     )
     for iteration in range(ITERS):
-        scaling, partial = called(
+        last = iteration == ITERS - 1
+        results = called(
             column_kernel,
-            [line, line],
-            [
-                listed, arrivals((1,)), square,
-                pltpu.VMEM((target_blocks, 8, frames), f32), square, square, flat,
-            ],
-            count, near_pairs, source_mass, *kept, over_tgt(partial),
+            [flat, flat] if last else [flat],
+            [flat][last:]
+            + [square, pltpu.VMEM((target_blocks, 8, frames), f32), square, square, flat],
+            count, pairs, source_mass, *kept, over_tgt(partial),
         )
+        partial, scaling = results[0], results[-1]
         gathered = over_src(partial)
-        if iteration < ITERS - 1:
+        if not last:
             (partial,) = called(
                 row_kernel,
                 [many],
-                [listed, arrivals((1,)), flat, flat, square, square, flat],
-                count, near_pairs, target_mass, *kept, gathered,
+                [flat, flat, square, square, flat],
+                count, pairs, target_mass, *kept, gathered,
             )
     potential = target_mass - log_sum_exp([gathered[k] for k in range(gathered.shape[0])])
     return scaling, potential

time: 179 us -> 200 us (1.12)
  the two profiles are of different devices: /device:TPU:28 before, /device:TPU:36 now
where the time goes in v5:
time: 200 us; the launch traced here: 199 us
  blocking collectives  107 us (54%)
  starting transfers between devices  56.2 us (28%)
  Pallas kernels  16.8 us (8%)
  waiting for transfers between devices  13.9 us (7%)
  local copies, waits for them, and re-layouts  2.99 us (1%)
    all_to_all x3, blocking collectives, exchanged(): return lax.all_to_all(x, axis, 0, 0, tiled=True)  77.5 us
    all_to_all x2, starting transfers between devices, exchanged(): return lax.all_to_all(x, axis, 0, 0, tiled=True)  56.2 us
    all_gather x1, blocking collectives, on_device(): lax.all_gather(jnp.swapaxes(source_embed, 1, 2), 'tgt')  23.9 us
    pallas_call x4, Pallas kernels, called(): pl.pallas_call(body, out_shape=outs, in_specs=[pl.BlockSpec(memory_space=...  16.8 us
    all_to_all x2, waiting for transfers between devices, exchanged(): return lax.all_to_all(x, axis, 0, 0, tiled=True)  13.9 us
  transfers between devices with their start and end apart: 2, of which 1 were waited for; matrix products, arithmetic and copies ran while one was open for 0% of the time, Pallas kernels for 0%

profile of v5, /device:TPU:36, one launch (start us, length us, event | category | flops | bytes accessed | tf_op | source)
XLA Modules:
  0.0 199.1 jit_solution(18211375061197101413)
XLA Ops:
  0.6 0.7 copy.9
  1.4 0.8 broadcast_in_dim.10
  2.1 15.2 %all-to-all-start = ((bf16[16,16,4,128]{3,1,2,0:T(8,128)(2,1)}), bf16[16,16,4,128]{3,1,2,0:T(8,128)(2,1)S(1)}, u32[]{:S(2)}, u32[]{:S(2)}) async-start(bf16[16,16,4,128]{3,1,2,0:T(8,128)(2,1)} %broadcast_in_dim.10), calls=%async_computation | async-start | bytes 524288 | tf_op jit(solution)/shard_map/all_to_all | solution.py:268
  18.0 23.9 %all-gather = bf16[256,8,128]{2,1,0:T(8,128)(2,1)S(1)} all-gather(bf16[16,8,128]{2,1,0:T(8,128)(2,1)} %bitcast.98), channel_id=2, replica_groups=mesh['z'=16,'c'=2,'tgt'=16] {'tgt'}, dimensions={0}, use_global_device_ids=true | all-gather | bytes 557056 | tf_op jit(solution)/shard_map/all_gather | solution.py:332
  41.9 0.0 all-to-all-done
  41.9 2.2 %all-gather.1 = bf16[32,16,4,128]{3,1,2,0:T(8,128)(2,1)S(1)} all-gather(bf16[16,16,4,128]{3,1,2,0:T(8,128)(2,1)S(1)} %all-to-all-done), channel_id=3, replica_groups=mesh['z'=16,'c'=2,'tgt'=16] {'c'}, dimensions={0}, use_global_device_ids=true | all-gather | bytes 786432 | tf_op jit(solution)/shard_map/all_gather | solution.py:333
  44.1 0.2 copy.10
  44.3 5.0 %shard_map.86 = (f32[128,128,128]{2,1,0:T(8,128)S(1)}, bf16[16,128,128]{2,1,0:T(8,128)(2,1)S(1)}, bf16[16,128,128]{2,1,0:T(8,128)(2,1)S(1)}, s32[2,128]{1,0:T(2,...) custom-call(s32[1]{0:T(128)} %bitcast.92.count_ref, s32[2,128]{1,0:T(2,128)} %bitcast.100, ...), custom_call_target="tpu_custom_call" | custom-call | tf_op jit(solution)/shard_map/pallas_call | solution.py:242
  49.3 10.4 %all_to_all.25.gathered = f32[16,16,128]{2,1,0:T(8,128)S(1)} all-to-all(f32[16,16,128]{2,1,0:T(8,128)S(1)} %get-tuple-element.17), channel_id=1, replica_groups=mesh['z'=16,'c'=2,'tgt'=16] {'tgt'}, dimensions={0} | all-to-all | bytes 262144 | tf_op jit(solution)/shard_map/all_to_all | solution.py:268
  59.7 3.9 %shard_map.87 = f32[16,128]{1,0:T(8,128)S(1)} custom-call(s32[1]{0:T(128)} %bitcast.93.count_ref, s32[2,128]{1,0:T(2,128)S(4)} %get-tuple-element.11.pairs, f32[16,128]{1,0:T(8,128)S(1)} %get-tuple-element.12.mass, f32[128,128,128]{2,1,0:T(8,128)S(1)} %get-tuple-element.13.cached, bf16[16,128,128]{2,1,0:T(8,128)(2,1)S(1)} %get-tuple-element.14.rows, ...), custom_call_target="tpu_custom_call" | custom-call | tf_op jit(solution)/shard_map/pallas_call | solution.py:242
  63.6 1.8 all-gather.2
  65.4 56.8 %all_to_all.26.gathered = f32[16,16,128]{2,1,0:T(8,128)S(1)} all-to-all(f32[16,16,128]{2,1,0:T(8,128)S(1)} %broadcast_in_dim.24), channel_id=1, replica_groups=mesh['z'=16,'c'=2,'tgt'=16] {'z'}, dimensions={0} | all-to-all | bytes 262144 | tf_op jit(solution)/shard_map/all_to_all | solution.py:268
  122.2 4.0 %shard_map.88 = f32[16,16,128]{2,1,0:T(8,128)S(1)} custom-call(s32[1]{0:T(128)} %bitcast.94.count_ref, s32[2,128]{1,0:T(2,128)S(4)} %get-tuple-element.11.pairs, f32[16,128]{1,0:T(8,128)S(1)} %get-tuple-element.16.mass, f32[128,128,128]{2,1,0:T(8,128)S(1)} %get-tuple-element.13.cached, bf16[16,128,128]{2,1,0:T(8,128)(2,1)S(1)} %get-tuple-element.14.rows, ...), custom_call_target="tpu_custom_call" | custom-call | tf_op jit(solution)/shard_map/pallas_call | solution.py:242
  126.3 10.4 %all_to_all.27.gathered = f32[16,16,128]{2,1,0:T(8,128)S(1)} all-to-all(f32[16,16,128]{2,1,0:T(8,128)S(1)} %shard_map.88), channel_id=1, replica_groups=mesh['z'=16,'c'=2,'tgt'=16] {'tgt'}, dimensions={0} | all-to-all | bytes 262144 | tf_op jit(solution)/shard_map/all_to_all | solution.py:268
  136.7 3.9 %shard_map.89 = (f32[16,128]{1,0:T(8,128)S(1)}, f32[16,128]{1,0:T(8,128)S(1)}) custom-call(s32[1]{0:T(128)} %bitcast.95.count_ref, s32[2,128]{1,0:T(2,128)S(4)} %get-tuple-element.11.pairs, f32[16,128]{1,0:T(8,128)S(1)} %get-tuple-element.12.mass, f32[128,128,128]{2,1,0:T(8,128)S(1)} %get-tuple-element.13.cached, ...), custom_call_target="tpu_custom_call" | custom-call | tf_op jit(solution)/shard_map/pallas_call | solution.py:242
  140.5 1.8 all-gather.3
  142.3 0.7 broadcast_in_dim.26
  143.0 41.0 %all-to-all-start.4 = ((f32[16,16,128]{2,1,0:T(8,128)}), f32[16,16,128]{2,1,0:T(8,128)S(1)}, u32[]{:S(2)}, u32[]{:S(2)}) async-start(f32[16,16,128]{2,1,0:T(8,128)} %broadcast_in_dim.26), calls=%async_computation.4 | async-start | bytes 262144 | tf_op jit(solution)/shard_map/all_to_all | solution.py:268
  184.0 0.6 copy.11
  184.6 13.9 %all-to-all-done.4 = f32[16,16,128]{2,1,0:T(8,128)S(1)} async-done(((f32[16,16,128]{2,1,0:T(8,128)}), f32[16,16,128]{2,1,0:T(8,128)S(1)}, u32[]{:S(2)}, u32[]{:S(2)}) %all-to-all-start.4) | async-done | bytes 131104 | tf_op jit(solution)/shard_map/all_to_all | solution.py:268
  198.5 0.7 add_subtract_fusion
  (3 shorter events, 0.0 us)
Async XLA Ops:
  2.1 39.8 %all-to-all-start = ((bf16[16,16,4,128]{3,1,2,0:T(8,128)(2,1)}), bf16[16,16,4,128]{3,1,2,0:T(8,128)(2,1)S(1)}, u32[]{:S(2)}, u32[]{:S(2)}) async-start(bf16[16,16,4,128]{3,1,2,0:T(8,128)(2,1)} %broadcast_in_dim.10), calls=%async_computation | async-start | bytes 524288 | tf_op jit(solution)/shard_map/all_to_all | solution.py:268
  143.0 55.5 %all-to-all-start.4 = ((f32[16,16,128]{2,1,0:T(8,128)}), f32[16,16,128]{2,1,0:T(8,128)S(1)}, u32[]{:S(2)}, u32[]{:S(2)}) async-start(f32[16,16,128]{2,1,0:T(8,128)} %broadcast_in_dim.26), calls=%async_computation.4 | async-start | bytes 262144 | tf_op jit(solution)/shard_map/all_to_all | solution.py:268

commit v6 on v5

--- a/solution.py
+++ b/solution.py
@@ -11,6 +11,7 @@
 
 ITERS = 2
 SRC = ("z", "c")
+TGT = ("y", "x")
 
 smoothing_epsilon = 4.0
 empty_peak = -1e30
@@ -159,11 +160,13 @@
         wide_source[:, pl.ds(device * features, features), :] = source[device].astype(
             jnp.float32
         )
-    cores, rings, _, parts, _ = target.shape
+    cores, rings, lines, frames = target.shape
+    parts = lines // blocks
     for ring in range(rings):
         for core in range(cores):
             at = (ring * cores + core) * parts
-            wide_target[:, pl.ds(at, parts), :] = target[core, ring].astype(jnp.float32)
+            piece = target[core, ring].astype(jnp.float32)
+            wide_target[:, pl.ds(at, parts), :] = piece.reshape(blocks, parts, frames)
     for block in range(blocks):
         rows[block] = wide_source[block].T.astype(jnp.bfloat16)
         columns[block] = wide_target[block].astype(jnp.bfloat16)
@@ -184,12 +187,13 @@
 
 
 def column_kernel(
-    count_ref, pairs, mass, cached, rows, columns, gathered, partial, scaling,
-    wide, slim, total, peak, sums,
+    count_ref, pairs, mass, cached, rows, columns, gathered, partial, *refs,
 ):
+    *result, scaling, wide, slim, total, peak, sums, arrived = refs
     count = count_ref[0]
     reached = log_sum_exp([gathered[k] for k in range(gathered.shape[0])])
     scaling[...] = mass[...] - reached
+    moves = fetches([scaling] * len(result), result, arrived)
     weights = jnp.exp(scaling[...])
     for block in range(wide.shape[0]):
         wide[block] = jnp.broadcast_to(weights[block : block + 1, :], wide.shape[1:]).T
@@ -214,6 +218,8 @@
         exact_columns(count, pairs, rows, columns, scaling, wide, peak, total, sums)
 
     partial[...] = sums[...]
+    for move in moves:
+        move.wait()
 
 
 def row_kernel(
@@ -229,6 +235,11 @@
     )
 
 
+def spaces_of(out):
+    space = getattr(out, "memory_space", pltpu.VMEM)
+    return pl.ANY if space == pltpu.HBM else space
+
+
 def called(body, outs, scratch, *operands, far=0):
     count, *rest = operands
     places = [
@@ -236,15 +247,12 @@
         for k, x in enumerate(rest)
     ]
     held = [pltpu.with_memory_space_constraint(x, place) for x, place in zip(rest, places)]
-    given = [
-        pltpu.SMEM if jnp.issubdtype(x.dtype, jnp.integer) else pltpu.VMEM for x in outs
-    ]
     return pl.pallas_call(
         body,
         out_shape=outs,
         in_specs=[pl.BlockSpec(memory_space=pltpu.SMEM)]
         + [pl.BlockSpec(memory_space=pl.ANY if x is pltpu.HBM else x) for x in places],
-        out_specs=[pl.BlockSpec(memory_space=x) for x in given],
+        out_specs=[pl.BlockSpec(memory_space=spaces_of(x)) for x in outs],
         scratch_shapes=scratch,
         compiler_params=pltpu.CompilerParams(vmem_limit_bytes=40 * 1024 * 1024),
     )(count, *held)
@@ -272,8 +280,8 @@
     f32, bf16 = jnp.float32, jnp.bfloat16
     slots = pairs.shape[1]
     across, source_blocks, depth, frames = source.shape
-    target_blocks = target.shape[2]
     features = across * depth
+    target_blocks = target.shape[0] * target.shape[1] * target.shape[2] // features
     many = jax.ShapeDtypeStruct((across, source_blocks, frames), f32)
     square = pltpu.VMEM((source_blocks, frames, frames), f32)
     flat = pltpu.VMEM((source_blocks, frames), f32)
@@ -300,9 +308,11 @@
         last = iteration == ITERS - 1
         results = called(
             column_kernel,
-            [flat, flat] if last else [flat],
-            [flat][last:]
-            + [square, pltpu.VMEM((target_blocks, 8, frames), f32), square, square, flat],
+            [flat, pltpu.HBM((source_blocks, frames), f32)] if last else [flat],
+            [
+                flat, square, pltpu.VMEM((target_blocks, 8, frames), f32), square, square,
+                flat, arrivals((1,)),
+            ],
             count, pairs, source_mass, *kept, over_tgt(partial),
         )
         partial, scaling = results[0], results[-1]
@@ -323,34 +333,70 @@
     return exchanged(copies(log_sum_exp([both[0], both[1]]), "z"), "z")
 
 
+def copying_kernel(source, target, sources, targets, near, arrived):
+    moves = fetches([source] * sources.shape[0] + [target], [*sources_of(sources), near], arrived)
+    moves[-1].wait()
+    flat = near[...].astype(jnp.float32).reshape(targets.shape[1:]).astype(targets.dtype)
+    targets[...] = jnp.broadcast_to(flat[None], targets.shape)
+    for move in moves[:-1]:
+        move.wait()
+
+
+def sources_of(ref):
+    return [ref.at[k] for k in range(ref.shape[0])]
+
+
+def copies_of_both(source, target):
+    across, rings = lax.axis_size("x"), lax.axis_size("z")
+    lines = target.shape[0] * target.shape[1]
+    return pl.pallas_call(
+        copying_kernel,
+        out_shape=[
+            jax.ShapeDtypeStruct((across, *source.shape), source.dtype),
+            jax.ShapeDtypeStruct((rings, lines, target.shape[2]), target.dtype),
+        ],
+        in_specs=[pl.BlockSpec(memory_space=pl.ANY)] * 2,
+        out_specs=[
+            pl.BlockSpec(memory_space=pl.ANY),
+            pl.BlockSpec(memory_space=pltpu.VMEM),
+        ],
+        scratch_shapes=[
+            pltpu.VMEM(target.shape, target.dtype),
+            pltpu.SemaphoreType.DMA((across + 1,)),
+        ],
+    )(*(pltpu.with_memory_space_constraint(one, pltpu.HBM) for one in (source, target)))
+
+
 def on_device(
     source_embed, target_embed, source_mass, target_mass, target_start, block_pairs, counts
 ):
     pairs = block_pairs.reshape(block_pairs.shape[2], 2).T
-    columns = exchanged(copies(jnp.swapaxes(target_embed, 1, 2), "z"), "z")
+    sources, targets = copies_of_both(
+        jnp.swapaxes(source_embed, 1, 2), jnp.swapaxes(target_embed, 1, 2)
+    )
+    source = lax.all_gather(exchanged(sources, "x"), "y", tiled=True)
+    target = lax.all_gather(exchanged(targets, "z"), "c")
     return local_chain(
-        lax.all_gather(jnp.swapaxes(source_embed, 1, 2), "tgt"),
-        lax.all_gather(columns, "c"),
-        target_start, source_mass, target_mass, pairs, counts.reshape(1),
-        lambda partial: exchanged(partial, "tgt"), over_src,
+        source, target, target_start, source_mass, target_mass, pairs, counts.reshape(1),
+        lambda partial: exchanged(partial, TGT), over_src,
     )
 
 
 def solution(mesh):
-    split = Mesh(mesh.devices.reshape(16, 2, mesh.shape["tgt"]), ("z", "c", "tgt"))
+    split = Mesh(mesh.devices.reshape(16, 2, 4, 4), (*SRC, *TGT))
     placed = (
-        P(SRC, None, "tgt"),
-        P("tgt", None, SRC),
+        P(SRC, None, TGT),
+        P(TGT, None, SRC),
         P(SRC, None),
-        P("tgt", None),
-        P("tgt", None),
-        P(SRC, "tgt", None, None),
-        P(SRC, "tgt"),
+        P(TGT, None),
+        P(TGT, None),
+        P(SRC, TGT, None, None),
+        P(SRC, TGT),
     )
     return jax.shard_map(
         on_device,
         mesh=split,
         in_specs=placed,
-        out_specs=(P(SRC, None), P("tgt", None)),
+        out_specs=(P(SRC, None), P(TGT, None)),
         check_vma=False,
     )

time: 200 us -> 194 us (0.970)
  the two profiles are of different devices: /device:TPU:36 before, /device:TPU:10 now
where the time goes in v6:
time: 194 us
  blocking collectives  157 us (81%)
  Pallas kernels  16 us (8%)
  starting transfers between devices  15.2 us (8%)
  waiting for transfers between devices  3.63 us (2%)
    all_to_all x5, blocking collectives, exchanged(): return lax.all_to_all(x, axis, 0, 0, tiled=True)  104 us
    all_gather x2, blocking collectives, over_src(): both = lax.all_gather(partial, 'c')  37.6 us
    all_to_all x1, starting transfers between devices, exchanged(): return lax.all_to_all(x, axis, 0, 0, tiled=True)  15.2 us
    all_gather x1, blocking collectives, on_device(): source = lax.all_gather(exchanged(sources, 'x'), 'y', tiled=True)  13 us
    pallas_call x4, Pallas kernels, called(): pl.pallas_call(body, out_shape=outs, in_specs=[pl.BlockSpec(memory_space=...  10.2 us
    pallas_call x1, Pallas kernels, copies_of_both(): pl.pallas_call(copying_kernel, out_shape=[jax.ShapeDtypeStruct((across, *...  5.81 us
  transfers between devices with their start and end apart: 1, of which 1 were waited for; matrix products, arithmetic and copies ran while one was open for 0% of the time, Pallas kernels for 0%

profile of v6, /device:TPU:10, one launch (start us, length us, event | category | flops | bytes accessed | tf_op | source)
XLA Modules:
  0.0 193.8 jit_solution(8213172101506465638)
XLA Ops:
  0.6 5.8 %shard_map.86 = (bf16[4,16,8,128]{3,2,1,0:T(8,128)(2,1)}, bf16[16,64,128]{2,1,0:T(8,128)(2,1)}) custom-call(bf16[16,8,128]{2,1,0:T(8,128)(2,1)} %bitcast.96, bf16[16,4,128]{2,1,0:T(4,128)(2,1)} %bitcast.97), custom_call_target="tpu_custom_call" | custom-call | tf_op jit(solution)/shard_map/pallas_call | solution.py:352
  6.4 9.4 %all_to_all.30 = bf16[4,16,8,128]{3,2,1,0:T(8,128)(2,1)S(1)} all-to-all(bf16[4,16,8,128]{3,2,1,0:T(8,128)(2,1)} %get-tuple-element.13), channel_id=1, replica_groups=mesh['z'=16,'c'=2,'y'=4,'x'=4] {'x'}, dimensions={0} | all-to-all | bytes 262144 | tf_op jit(solution)/shard_map/all_to_all | solution.py:276
  15.8 15.2 %all-to-all-start.1 = ((bf16[16,64,128]{2,1,0:T(8,128)(2,1)}), bf16[16,64,128]{2,1,0:T(8,128)(2,1)S(1)}, u32[]{:S(2)}, u32[]{:S(2)}) async-start(bf16[16,64,128]{2,1,0:T(8,128)(2,1)} %get-tuple-element.14), calls=%async_computation.1 | async-start | bytes 524288 | tf_op jit(solution)/shard_map/all_to_all | solution.py:276
  31.6 13.0 %all_gather.21.source = bf16[16,16,8,128]{3,2,1,0:T(8,128)(2,1)S(1)} all-gather(bf16[4,16,8,128]{3,2,1,0:T(8,128)(2,1)S(1)} %all_to_all.30), channel_id=1, replica_groups=mesh['z'=16,'c'=2,'y'=4,'x'=4] {'y'}, dimensions={0}, use_global_device_ids=true | all-gather | bytes 655360 | tf_op jit(solution)/shard_map/all_gather | solution.py:377
  44.7 3.6 %all-to-all-done.1 = bf16[16,64,128]{2,1,0:T(8,128)(2,1)S(1)} async-done(((bf16[16,64,128]{2,1,0:T(8,128)(2,1)}), bf16[16,64,128]{2,1,0:T(8,128)(2,1)S(1)}, u32[]{:S(2)}, u32[]{:S(2)}) %all-to-all-start.1) | async-done | bytes 262176 | tf_op jit(solution)/shard_map/all_to_all | solution.py:276
  48.3 2.2 %all-gather = bf16[32,64,128]{2,1,0:T(8,128)(2,1)S(1)} all-gather(bf16[16,64,128]{2,1,0:T(8,128)(2,1)S(1)} %all-to-all-done.1), channel_id=2, replica_groups=mesh['z'=16,'c'=2,'y'=4,'x'=4] {'c'}, dimensions={0}, use_global_device_ids=true | all-gather | bytes 786432 | tf_op jit(solution)/shard_map/all_gather | solution.py:378
  50.5 1.6 shard_map.87
  52.1 13.8 %all_to_all.31.gathered = f32[16,16,128]{2,1,0:T(8,128)S(1)} all-to-all(f32[16,16,128]{2,1,0:T(8,128)S(1)} %get-tuple-element.21), channel_id=1, replica_groups=mesh['z'=16,'c'=2,'y'=4,'x'=4] {'y','x'}, dimensions={0} | all-to-all | bytes 262144 | tf_op jit(solution)/shard_map/all_to_all | solution.py:276
  65.9 3.9 %shard_map.88 = f32[16,128]{1,0:T(8,128)S(1)} custom-call(s32[1]{0:T(128)} %bitcast.92.count_ref, s32[2,128]{1,0:T(2,128)S(4)} %get-tuple-element.15.pairs, f32[16,128]{1,0:T(8,128)S(1)} %get-tuple-element.16.mass, f32[128,128,128]{2,1,0:T(8,128)S(1)} %get-tuple-element.17.cached, bf16[16,128,128]{2,1,0:T(8,128)(2,1)S(1)} %get-tuple-element.18.rows, ...), custom_call_target="tpu_custom_call" | custom-call | tf_op jit(solution)/shard_map/pallas_call | solution.py:250
  69.8 21.2 %all-gather.1 = f32[32,128]{1,0:T(8,128)S(1)} all-gather(f32[16,128]{1,0:T(8,128)S(1)} %shard_map.88), channel_id=3, replica_groups=mesh['z'=16,'c'=2,'y'=4,'x'=4] {'c'}, dimensions={0}, use_global_device_ids=true | all-gather | bytes 24576 | tf_op jit(solution)/shard_map/all_gather | solution.py:332
  91.1 33.3 %all_to_all.32.gathered = f32[16,16,128]{2,1,0:T(8,128)S(1)} all-to-all(f32[16,16,128]{2,1,0:T(8,128)S(1)} %broadcast_in_dim.17), channel_id=1, replica_groups=mesh['z'=16,'c'=2,'y'=4,'x'=4] {'z'}, dimensions={0} | all-to-all | bytes 262144 | tf_op jit(solution)/shard_map/all_to_all | solution.py:276
  124.4 0.7 shard_map.89
  125.1 11.3 %all_to_all.33.gathered = f32[16,16,128]{2,1,0:T(8,128)S(1)} all-to-all(f32[16,16,128]{2,1,0:T(8,128)S(1)} %shard_map.89), channel_id=1, replica_groups=mesh['z'=16,'c'=2,'y'=4,'x'=4] {'y','x'}, dimensions={0} | all-to-all | bytes 262144 | tf_op jit(solution)/shard_map/all_to_all | solution.py:276
  136.4 3.9 %shard_map.90 = (f32[16,128]{1,0:T(8,128)S(1)}, f32[16,128]{1,0:T(8,128)}) custom-call(s32[1]{0:T(128)} %bitcast.94.count_ref, s32[2,128]{1,0:T(2,128)S(4)} %get-tuple-element.15.pairs, f32[16,128]{1,0:T(8,128)S(1)} %get-tuple-element.16.mass, f32[128,128,128]{2,1,0:T(8,128)S(1)} %get-tuple-element.17.cached, ...), custom_call_target="tpu_custom_call" | custom-call | tf_op jit(solution)/shard_map/pallas_call | solution.py:250
  140.4 16.4 %all-gather.2 = f32[32,128]{1,0:T(8,128)S(1)} all-gather(f32[16,128]{1,0:T(8,128)S(1)} %get-tuple-element.23), channel_id=4, replica_groups=mesh['z'=16,'c'=2,'y'=4,'x'=4] {'c'}, dimensions={0}, use_global_device_ids=true | all-gather | bytes 24576 | tf_op jit(solution)/shard_map/all_gather | solution.py:332
  156.8 36.4 %all_to_all.34 = f32[16,16,128]{2,1,0:T(8,128)S(1)} all-to-all(f32[16,16,128]{2,1,0:T(8,128)S(1)} %broadcast_in_dim.19), channel_id=1, replica_groups=mesh['z'=16,'c'=2,'y'=4,'x'=4] {'z'}, dimensions={0} | all-to-all | bytes 262144 | tf_op jit(solution)/shard_map/all_to_all | solution.py:276
  193.1 0.7 add_subtract_fusion
  (4 shorter events, 0.1 us)
Async XLA Ops:
  15.8 32.5 %all-to-all-start.1 = ((bf16[16,64,128]{2,1,0:T(8,128)(2,1)}), bf16[16,64,128]{2,1,0:T(8,128)(2,1)S(1)}, u32[]{:S(2)}, u32[]{:S(2)}) async-start(bf16[16,64,128]{2,1,0:T(8,128)(2,1)} %get-tuple-element.14), calls=%async_computation.1 | async-start | bytes 524288 | tf_op jit(solution)/shard_map/all_to_all | solution.py:276

commit v7 on v6

--- a/solution.py
+++ b/solution.py
@@ -144,35 +144,38 @@
     spread(partial, sums)
 
 
-def first_kernel(
-    count_ref, far_pairs, far_start, far_source_mass, far_target_mass, source, target,
-    cached, rows, columns, pairs, source_mass, target_mass, partial,
-    start, arrived, wide_source, wide_target, weights, total, peak, sums,
+def source_kernel(
+    far_pairs, far_start, far_source_mass, far_target_mass, source,
+    rows, pairs, start, source_mass, target_mass, wide, arrived,
 ):
     moves = fetches(
         (far_pairs, far_start, far_source_mass, far_target_mass),
         (pairs, start, source_mass, target_mass),
         arrived,
     )
-    blocks = source.shape[1]
     features = source.shape[2]
     for device in range(source.shape[0]):
-        wide_source[:, pl.ds(device * features, features), :] = source[device].astype(
-            jnp.float32
-        )
+        wide[:, pl.ds(device * features, features), :] = source[device].astype(jnp.float32)
+    for block in range(source.shape[1]):
+        rows[block] = wide[block].T.astype(rows.dtype)
+    for move in moves:
+        move.wait()
+
+
+def first_kernel(
+    count_ref, pairs, start, rows, target, cached, columns, partial,
+    wide, weights, total, peak, sums,
+):
     cores, rings, lines, frames = target.shape
+    blocks = columns.shape[0]
     parts = lines // blocks
     for ring in range(rings):
         for core in range(cores):
             at = (ring * cores + core) * parts
             piece = target[core, ring].astype(jnp.float32)
-            wide_target[:, pl.ds(at, parts), :] = piece.reshape(blocks, parts, frames)
+            wide[:, pl.ds(at, parts), :] = piece.reshape(blocks, parts, frames)
     for block in range(blocks):
-        rows[block] = wide_source[block].T.astype(jnp.bfloat16)
-        columns[block] = wide_target[block].astype(jnp.bfloat16)
-
-    for move in moves[:2]:
-        move.wait()
+        columns[block] = wide[block].astype(columns.dtype)
 
     def kernel_of(slot, source, target):
         value = jnp.exp2(scores(rows[source], columns[target]) * to_log2)
@@ -180,10 +183,9 @@
         return value
 
     row_pass(
-        group, count_ref[0], pairs, rows, columns, start, kernel_of, weights, total, peak, sums, partial
-    )
-    for move in moves[2:]:
-        move.wait()
+        group, count_ref[0], pairs, rows, columns, start, kernel_of,
+        weights, total, peak, sums, partial,
+    )
 
 
 def column_kernel(
@@ -241,21 +243,22 @@
 
 
 def called(body, outs, scratch, *operands, far=0):
-    count, *rest = operands
     places = [
         pltpu.HBM if k < far else pltpu.SMEM if jnp.issubdtype(x.dtype, jnp.integer) else pltpu.VMEM
-        for k, x in enumerate(rest)
+        for k, x in enumerate(operands)
     ]
-    held = [pltpu.with_memory_space_constraint(x, place) for x, place in zip(rest, places)]
+    held = [
+        x if x.size == 1 else pltpu.with_memory_space_constraint(x, place)
+        for x, place in zip(operands, places)
+    ]
     return pl.pallas_call(
         body,
         out_shape=outs,
-        in_specs=[pl.BlockSpec(memory_space=pltpu.SMEM)]
-        + [pl.BlockSpec(memory_space=pl.ANY if x is pltpu.HBM else x) for x in places],
+        in_specs=[pl.BlockSpec(memory_space=pl.ANY if x is pltpu.HBM else x) for x in places],
         out_specs=[pl.BlockSpec(memory_space=spaces_of(x)) for x in outs],
         scratch_shapes=scratch,
         compiler_params=pltpu.CompilerParams(vmem_limit_bytes=40 * 1024 * 1024),
-    )(count, *held)
+    )(*held)
 
 
 def fetches(sources, places, arrived):
@@ -287,23 +290,27 @@
     flat = pltpu.VMEM((source_blocks, frames), f32)
     listed = pltpu.SMEM(pairs.shape, jnp.int32)
     arrivals = pltpu.SemaphoreType.DMA
-    *kept, pairs, source_mass, target_mass, partial = called(
+    rows, pairs, start, source_mass, target_mass = called(
+        source_kernel,
+        [pltpu.VMEM((source_blocks, frames, features), bf16), listed, flat, flat, flat],
+        [pltpu.VMEM((source_blocks, features, frames), f32), arrivals((4,))],
+        pairs, start, source_mass, target_mass, source,
+        far=4,
+    )
+    cached, columns, partial = called(
         first_kernel,
         [
             pltpu.VMEM((slots, frames, frames), f32),
-            pltpu.VMEM((source_blocks, frames, features), bf16),
             pltpu.VMEM((target_blocks, features, frames), bf16),
-            listed, flat, flat, many,
+            many,
         ],
         [
-            flat, arrivals((4,)),
-            pltpu.VMEM((source_blocks, features, frames), f32),
             pltpu.VMEM((target_blocks, features, frames), f32),
             flat, square, square, flat,
         ],
-        count, pairs, start, source_mass, target_mass, source, target,
-        far=4,
-    )
+        count, pairs, start, rows, target,
+    )
+    kept = [cached, rows, columns]
     for iteration in range(ITERS):
         last = iteration == ITERS - 1
         results = called(
@@ -333,36 +340,30 @@
     return exchanged(copies(log_sum_exp([both[0], both[1]]), "z"), "z")
 
 
-def copying_kernel(source, target, sources, targets, near, arrived):
-    moves = fetches([source] * sources.shape[0] + [target], [*sources_of(sources), near], arrived)
-    moves[-1].wait()
-    flat = near[...].astype(jnp.float32).reshape(targets.shape[1:]).astype(targets.dtype)
-    targets[...] = jnp.broadcast_to(flat[None], targets.shape)
-    for move in moves[:-1]:
+def copying_kernel(source, target, sources, targets, near_source, near_target, arrived):
+    moves = fetches((source, target), (near_source, near_target), arrived)
+    for move in moves:
         move.wait()
-
-
-def sources_of(ref):
-    return [ref.at[k] for k in range(ref.shape[0])]
+    sources[...] = jnp.broadcast_to(near_source[...][None], sources.shape)
+    flat = near_target[...].astype(jnp.float32).reshape(targets.shape[1:])
+    targets[...] = jnp.broadcast_to(flat.astype(targets.dtype)[None], targets.shape)
 
 
 def copies_of_both(source, target):
-    across, rings = lax.axis_size("x"), lax.axis_size("z")
+    across, rings = lax.axis_size(TGT), lax.axis_size("z")
     lines = target.shape[0] * target.shape[1]
     return pl.pallas_call(
         copying_kernel,
         out_shape=[
-            jax.ShapeDtypeStruct((across, *source.shape), source.dtype),
+            pltpu.VMEM((across, *source.shape), source.dtype),
             jax.ShapeDtypeStruct((rings, lines, target.shape[2]), target.dtype),
         ],
         in_specs=[pl.BlockSpec(memory_space=pl.ANY)] * 2,
-        out_specs=[
-            pl.BlockSpec(memory_space=pl.ANY),
-            pl.BlockSpec(memory_space=pltpu.VMEM),
-        ],
+        out_specs=[pl.BlockSpec(memory_space=pltpu.VMEM)] * 2,
         scratch_shapes=[
+            pltpu.VMEM(source.shape, source.dtype),
             pltpu.VMEM(target.shape, target.dtype),
-            pltpu.SemaphoreType.DMA((across + 1,)),
+            pltpu.SemaphoreType.DMA((2,)),
         ],
     )(*(pltpu.with_memory_space_constraint(one, pltpu.HBM) for one in (source, target)))
 
@@ -374,7 +375,7 @@
     sources, targets = copies_of_both(
         jnp.swapaxes(source_embed, 1, 2), jnp.swapaxes(target_embed, 1, 2)
     )
-    source = lax.all_gather(exchanged(sources, "x"), "y", tiled=True)
+    source = exchanged(sources, TGT)
     target = lax.all_gather(exchanged(targets, "z"), "c")
     return local_chain(
         source, target, target_start, source_mass, target_mass, pairs, counts.reshape(1),

time: 194 us -> 173 us (0.89)
  the two profiles are of different devices: /device:TPU:10 before, /device:TPU:8 now
where the time goes in v7:
time: 173 us; the launch traced here: 172 us
  blocking collectives  125 us (72%)
  waiting for transfers between devices  16.3 us (9%)
  starting transfers between devices  14.7 us (8%)
  Pallas kernels  14.3 us (8%)
    all_to_all x5, blocking collectives, exchanged(): return lax.all_to_all(x, axis, 0, 0, tiled=True)  119 us
    all_to_all x1, waiting for transfers between devices, exchanged(): return lax.all_to_all(x, axis, 0, 0, tiled=True)  16.3 us
    all_to_all x1, starting transfers between devices, exchanged(): return lax.all_to_all(x, axis, 0, 0, tiled=True)  14.7 us
    pallas_call x5, Pallas kernels, called(): pl.pallas_call(body, out_shape=outs, in_specs=[pl.BlockSpec(memory_space=...  12.6 us
    all_gather x2, blocking collectives, over_src(): both = lax.all_gather(partial, 'c')  3.63 us
  transfers between devices with their start and end apart: 1, of which 1 were waited for; matrix products, arithmetic and copies ran while one was open for 0% of the time, Pallas kernels for 0%

profile of v7, /device:TPU:8, one launch (start us, length us, event | category | flops | bytes accessed | tf_op | source)
XLA Modules:
  0.0 172.3 jit_solution(3241431242931981285)
XLA Ops:
  0.6 1.6 shard_map.86
  2.2 16.6 %all_to_all.30.source = bf16[16,16,8,128]{3,2,1,0:T(8,128)(2,1)S(1)} all-to-all(bf16[16,16,8,128]{3,2,1,0:T(8,128)(2,1)S(1)} %get-tuple-element.14), channel_id=1, replica_groups=mesh['z'=16,'c'=2,'y'=4,'x'=4] {'y','x'}, dimensions={0} | all-to-all | bytes 1048576 | tf_op jit(solution)/shard_map/all_to_all | solution.py:279
  18.9 14.7 %all-to-all-start.1 = ((bf16[16,64,128]{2,1,0:T(8,128)(2,1)}), bf16[16,64,128]{2,1,0:T(8,128)(2,1)S(1)}, u32[]{:S(2)}, u32[]{:S(2)}) async-start(bf16[16,64,128]{2,1,0:T(8,128)(2,1)} %get-tuple-element.19), calls=%async_computation.1 | async-start | bytes 524288 | tf_op jit(solution)/shard_map/all_to_all | solution.py:279
  34.2 0.8 shard_map.87
  35.0 16.3 %all-to-all-done.1 = bf16[16,64,128]{2,1,0:T(8,128)(2,1)S(1)} async-done(((bf16[16,64,128]{2,1,0:T(8,128)(2,1)}), bf16[16,64,128]{2,1,0:T(8,128)(2,1)S(1)}, u32[]{:S(2)}, u32[]{:S(2)}) %all-to-all-start.1) | async-done | bytes 262176 | tf_op jit(solution)/shard_map/all_to_all | solution.py:279
  51.3 2.2 %all-gather = bf16[32,64,128]{2,1,0:T(8,128)(2,1)S(1)} all-gather(bf16[16,64,128]{2,1,0:T(8,128)(2,1)S(1)} %all-to-all-done.1), channel_id=2, replica_groups=mesh['z'=16,'c'=2,'y'=4,'x'=4] {'c'}, dimensions={0}, use_global_device_ids=true | all-gather | bytes 786432 | tf_op jit(solution)/shard_map/all_gather | solution.py:379
  53.5 1.5 shard_map.88
  55.1 14.8 %all_to_all.31.gathered = f32[16,16,128]{2,1,0:T(8,128)S(1)} all-to-all(f32[16,16,128]{2,1,0:T(8,128)S(1)} %get-tuple-element.23), channel_id=1, replica_groups=mesh['z'=16,'c'=2,'y'=4,'x'=4] {'y','x'}, dimensions={0} | all-to-all | bytes 262144 | tf_op jit(solution)/shard_map/all_to_all | solution.py:279
  69.8 4.8 %shard_map.89 = f32[16,128]{1,0:T(8,128)S(1)} custom-call(s32[1]{0:T(128)} %bitcast.92.count_ref, s32[2,128]{1,0:T(2,128)S(4)} %get-tuple-element.15.pairs, f32[16,128]{1,0:T(8,128)S(1)} %get-tuple-element.16.mass, f32[128,128,128]{2,1,0:T(8,128)S(1)} %get-tuple-element.20.cached, bf16[16,128,128]{2,1,0:T(8,128)(2,1)S(1)} %get-tuple-element.18.rows, ...), custom_call_target="tpu_custom_call" | custom-call | tf_op jit(solution)/shard_map/pallas_call | solution.py:254
  74.6 1.8 %all-gather.1 = f32[32,128]{1,0:T(8,128)S(1)} all-gather(f32[16,128]{1,0:T(8,128)S(1)} %shard_map.89), channel_id=3, replica_groups=mesh['z'=16,'c'=2,'y'=4,'x'=4] {'c'}, dimensions={0}, use_global_device_ids=true | all-gather | bytes 24576 | tf_op jit(solution)/shard_map/all_gather | solution.py:339
  76.5 37.1 %all_to_all.32.gathered = f32[16,16,128]{2,1,0:T(8,128)S(1)} all-to-all(f32[16,16,128]{2,1,0:T(8,128)S(1)} %broadcast_in_dim.17), channel_id=1, replica_groups=mesh['z'=16,'c'=2,'y'=4,'x'=4] {'z'}, dimensions={0} | all-to-all | bytes 262144 | tf_op jit(solution)/shard_map/all_to_all | solution.py:279
  113.6 0.8 shard_map.90
  114.4 13.2 %all_to_all.33.gathered = f32[16,16,128]{2,1,0:T(8,128)S(1)} all-to-all(f32[16,16,128]{2,1,0:T(8,128)S(1)} %shard_map.90), channel_id=1, replica_groups=mesh['z'=16,'c'=2,'y'=4,'x'=4] {'y','x'}, dimensions={0} | all-to-all | bytes 262144 | tf_op jit(solution)/shard_map/all_to_all | solution.py:279
  127.5 4.8 %shard_map.91 = (f32[16,128]{1,0:T(8,128)S(1)}, f32[16,128]{1,0:T(8,128)}) custom-call(s32[1]{0:T(128)} %bitcast.94.count_ref, s32[2,128]{1,0:T(2,128)S(4)} %get-tuple-element.15.pairs, f32[16,128]{1,0:T(8,128)S(1)} %get-tuple-element.16.mass, f32[128,128,128]{2,1,0:T(8,128)S(1)} %get-tuple-element.20.cached, ...), custom_call_target="tpu_custom_call" | custom-call | tf_op jit(solution)/shard_map/pallas_call | solution.py:254
  132.3 1.8 %all-gather.2 = f32[32,128]{1,0:T(8,128)S(1)} all-gather(f32[16,128]{1,0:T(8,128)S(1)} %get-tuple-element.25), channel_id=4, replica_groups=mesh['z'=16,'c'=2,'y'=4,'x'=4] {'c'}, dimensions={0}, use_global_device_ids=true | all-gather | bytes 24576 | tf_op jit(solution)/shard_map/all_gather | solution.py:339
  134.2 37.4 %all_to_all.34 = f32[16,16,128]{2,1,0:T(8,128)S(1)} all-to-all(f32[16,16,128]{2,1,0:T(8,128)S(1)} %broadcast_in_dim.19), channel_id=1, replica_groups=mesh['z'=16,'c'=2,'y'=4,'x'=4] {'z'}, dimensions={0} | all-to-all | bytes 262144 | tf_op jit(solution)/shard_map/all_to_all | solution.py:279
  171.6 0.7 add_subtract_fusion
  (4 shorter events, 0.1 us)
Async XLA Ops:
  18.9 32.5 %all-to-all-start.1 = ((bf16[16,64,128]{2,1,0:T(8,128)(2,1)}), bf16[16,64,128]{2,1,0:T(8,128)(2,1)S(1)}, u32[]{:S(2)}, u32[]{:S(2)}) async-start(bf16[16,64,128]{2,1,0:T(8,128)(2,1)} %get-tuple-element.19), calls=%async_computation.1 | async-start | bytes 524288 | tf_op jit(solution)/shard_map/all_to_all | solution.py:279

commit v8 on v6

--- a/solution.py
+++ b/solution.py
@@ -145,7 +145,7 @@
 
 
 def first_kernel(
-    count_ref, far_pairs, far_start, far_source_mass, far_target_mass, source, target,
+    far_pairs, far_start, far_source_mass, far_target_mass, count_ref, source, target,
     cached, rows, columns, pairs, source_mass, target_mass, partial,
     start, arrived, wide_source, wide_target, weights, total, peak, sums,
 ):
@@ -180,7 +180,8 @@
         return value
 
     row_pass(
-        group, count_ref[0], pairs, rows, columns, start, kernel_of, weights, total, peak, sums, partial
+        group, count_ref[0], pairs, rows, columns, start, kernel_of,
+        weights, total, peak, sums, partial,
     )
     for move in moves[2:]:
         move.wait()
@@ -241,21 +242,22 @@
 
 
 def called(body, outs, scratch, *operands, far=0):
-    count, *rest = operands
     places = [
         pltpu.HBM if k < far else pltpu.SMEM if jnp.issubdtype(x.dtype, jnp.integer) else pltpu.VMEM
-        for k, x in enumerate(rest)
+        for k, x in enumerate(operands)
     ]
-    held = [pltpu.with_memory_space_constraint(x, place) for x, place in zip(rest, places)]
+    held = [
+        x if x.size == 1 else pltpu.with_memory_space_constraint(x, place)
+        for x, place in zip(operands, places)
+    ]
     return pl.pallas_call(
         body,
         out_shape=outs,
-        in_specs=[pl.BlockSpec(memory_space=pltpu.SMEM)]
-        + [pl.BlockSpec(memory_space=pl.ANY if x is pltpu.HBM else x) for x in places],
+        in_specs=[pl.BlockSpec(memory_space=pl.ANY if x is pltpu.HBM else x) for x in places],
         out_specs=[pl.BlockSpec(memory_space=spaces_of(x)) for x in outs],
         scratch_shapes=scratch,
         compiler_params=pltpu.CompilerParams(vmem_limit_bytes=40 * 1024 * 1024),
-    )(count, *held)
+    )(*held)
 
 
 def fetches(sources, places, arrived):
@@ -301,7 +303,7 @@
             pltpu.VMEM((target_blocks, features, frames), f32),
             flat, square, square, flat,
         ],
-        count, pairs, start, source_mass, target_mass, source, target,
+        pairs, start, source_mass, target_mass, count, source, target,
         far=4,
     )
     for iteration in range(ITERS):
@@ -333,49 +335,33 @@
     return exchanged(copies(log_sum_exp([both[0], both[1]]), "z"), "z")
 
 
-def copying_kernel(source, target, sources, targets, near, arrived):
-    moves = fetches([source] * sources.shape[0] + [target], [*sources_of(sources), near], arrived)
-    moves[-1].wait()
-    flat = near[...].astype(jnp.float32).reshape(targets.shape[1:]).astype(targets.dtype)
-    targets[...] = jnp.broadcast_to(flat[None], targets.shape)
-    for move in moves[:-1]:
-        move.wait()
-
-
-def sources_of(ref):
-    return [ref.at[k] for k in range(ref.shape[0])]
-
-
-def copies_of_both(source, target):
-    across, rings = lax.axis_size("x"), lax.axis_size("z")
-    lines = target.shape[0] * target.shape[1]
-    return pl.pallas_call(
+def copying_kernel(far, copied, near, arrived):
+    (move,) = fetches((far,), (near,), arrived)
+    move.wait()
+    lines = near[...].astype(jnp.float32).reshape(copied.shape[1:]).astype(copied.dtype)
+    copied[...] = jnp.broadcast_to(lines[None], copied.shape)
+
+
+def line_copies(x, axis):
+    blocks, features, frames = x.shape
+    lines = jax.ShapeDtypeStruct((lax.axis_size(axis), blocks * features, frames), x.dtype)
+    (copied,) = called(
         copying_kernel,
-        out_shape=[
-            jax.ShapeDtypeStruct((across, *source.shape), source.dtype),
-            jax.ShapeDtypeStruct((rings, lines, target.shape[2]), target.dtype),
-        ],
-        in_specs=[pl.BlockSpec(memory_space=pl.ANY)] * 2,
-        out_specs=[
-            pl.BlockSpec(memory_space=pl.ANY),
-            pl.BlockSpec(memory_space=pltpu.VMEM),
-        ],
-        scratch_shapes=[
-            pltpu.VMEM(target.shape, target.dtype),
-            pltpu.SemaphoreType.DMA((across + 1,)),
-        ],
-    )(*(pltpu.with_memory_space_constraint(one, pltpu.HBM) for one in (source, target)))
+        [lines],
+        [pltpu.VMEM(x.shape, x.dtype), pltpu.SemaphoreType.DMA((1,))],
+        x,
+        far=1,
+    )
+    return copied
 
 
 def on_device(
     source_embed, target_embed, source_mass, target_mass, target_start, block_pairs, counts
 ):
     pairs = block_pairs.reshape(block_pairs.shape[2], 2).T
-    sources, targets = copies_of_both(
-        jnp.swapaxes(source_embed, 1, 2), jnp.swapaxes(target_embed, 1, 2)
-    )
-    source = lax.all_gather(exchanged(sources, "x"), "y", tiled=True)
-    target = lax.all_gather(exchanged(targets, "z"), "c")
+    columns = exchanged(line_copies(jnp.swapaxes(target_embed, 1, 2), "z"), "z")
+    source = lax.all_gather(jnp.swapaxes(source_embed, 1, 2), TGT)
+    target = lax.all_gather(columns, "c")
     return local_chain(
         source, target, target_start, source_mass, target_mass, pairs, counts.reshape(1),
         lambda partial: exchanged(partial, TGT), over_src,

time: 194 us -> 185 us (0.954)
  the two profiles are of different devices: /device:TPU:10 before, /device:TPU:32 now
where the time goes in v8:
time: 185 us
  blocking collectives  142 us (77%)
  Pallas kernels  25.4 us (14%)
  starting transfers between devices  15.2 us (8%)
    all_to_all x4, blocking collectives, exchanged(): return lax.all_to_all(x, axis, 0, 0, tiled=True)  112 us
    pallas_call x5, Pallas kernels, called(): pl.pallas_call(body, out_shape=outs, in_specs=[pl.BlockSpec(memory_space=...  25.4 us
    all_gather x1, blocking collectives, on_device(): source = lax.all_gather(jnp.swapaxes(source_embed, 1, 2), TGT)  24.6 us
    all_to_all x1, starting transfers between devices, exchanged(): return lax.all_to_all(x, axis, 0, 0, tiled=True)  15.2 us
  transfers between devices with their start and end apart: 1, of which 0 were waited for; matrix products, arithmetic and copies ran while one was open for 0% of the time, Pallas kernels for 0%

profile of v8, /device:TPU:32, one launch (start us, length us, event | category | flops | bytes accessed | tf_op | source)
XLA Modules:
  0.0 184.8 jit_solution(17296664259871488700)
XLA Ops:
  0.6 1.4 shard_map.86
  2.1 15.2 %all-to-all-start = ((bf16[16,64,128]{2,1,0:T(8,128)(2,1)}), bf16[16,64,128]{2,1,0:T(8,128)(2,1)S(1)}, u32[]{:S(2)}, u32[]{:S(2)}) async-start(bf16[16,64,128]{2,1,0:T(8,128)(2,1)} %shard_map.86), calls=%async_computation | async-start | bytes 524288 | tf_op jit(solution)/shard_map/all_to_all | solution.py:278
  18.0 24.6 %all-gather = bf16[256,8,128]{2,1,0:T(8,128)(2,1)S(1)} all-gather(bf16[16,8,128]{2,1,0:T(8,128)(2,1)} %bitcast.98), channel_id=2, replica_groups=mesh['z'=16,'c'=2,'y'=4,'x'=4] {'y','x'}, dimensions={0}, use_global_device_ids=true | all-gather | bytes 557056 | tf_op jit(solution)/shard_map/all_gather | solution.py:363
  42.5 0.0 all-to-all-done
  42.5 2.2 %all-gather.1 = bf16[32,64,128]{2,1,0:T(8,128)(2,1)S(1)} all-gather(bf16[16,64,128]{2,1,0:T(8,128)(2,1)S(1)} %all-to-all-done), channel_id=3, replica_groups=mesh['z'=16,'c'=2,'y'=4,'x'=4] {'c'}, dimensions={0}, use_global_device_ids=true | all-gather | bytes 786432 | tf_op jit(solution)/shard_map/all_gather | solution.py:364
  44.7 2.7 %shard_map.87 = (f32[128,128,128]{2,1,0:T(8,128)S(1)}, bf16[16,128,128]{2,1,0:T(8,128)(2,1)S(1)}, bf16[16,128,128]{2,1,0:T(8,128)(2,1)S(1)}, s32[2,128]{1,0:T(2,...) custom-call(s32[2,128]{1,0:T(2,128)} %bitcast.100, f32[16,128]{1,0:T(8,128)} %far_start.1, ...), custom_call_target="tpu_custom_call" | custom-call | tf_op jit(solution)/shard_map/pallas_call | solution.py:253
  47.4 14.7 %all_to_all.25.gathered = f32[16,16,128]{2,1,0:T(8,128)S(1)} all-to-all(f32[16,16,128]{2,1,0:T(8,128)S(1)} %get-tuple-element.17), channel_id=1, replica_groups=mesh['z'=16,'c'=2,'y'=4,'x'=4] {'y','x'}, dimensions={0} | all-to-all | bytes 262144 | tf_op jit(solution)/shard_map/all_to_all | solution.py:278
  62.1 10.1 %shard_map.88 = f32[16,128]{1,0:T(8,128)S(1)} custom-call(s32[1]{0:T(128)} %bitcast.93.count_ref, s32[2,128]{1,0:T(2,128)S(4)} %get-tuple-element.11.pairs, f32[16,128]{1,0:T(8,128)S(1)} %get-tuple-element.12.mass, f32[128,128,128]{2,1,0:T(8,128)S(1)} %get-tuple-element.13.cached, bf16[16,128,128]{2,1,0:T(8,128)(2,1)S(1)} %get-tuple-element.14.rows, ...), custom_call_target="tpu_custom_call" | custom-call | tf_op jit(solution)/shard_map/pallas_call | solution.py:253
  72.2 1.8 all-gather.2
  74.1 41.7 %all_to_all.26.gathered = f32[16,16,128]{2,1,0:T(8,128)S(1)} all-to-all(f32[16,16,128]{2,1,0:T(8,128)S(1)} %broadcast_in_dim.17), channel_id=1, replica_groups=mesh['z'=16,'c'=2,'y'=4,'x'=4] {'z'}, dimensions={0} | all-to-all | bytes 262144 | tf_op jit(solution)/shard_map/all_to_all | solution.py:278
  115.7 1.1 shard_map.89
  116.8 10.6 %all_to_all.27.gathered = f32[16,16,128]{2,1,0:T(8,128)S(1)} all-to-all(f32[16,16,128]{2,1,0:T(8,128)S(1)} %shard_map.89), channel_id=1, replica_groups=mesh['z'=16,'c'=2,'y'=4,'x'=4] {'y','x'}, dimensions={0} | all-to-all | bytes 262144 | tf_op jit(solution)/shard_map/all_to_all | solution.py:278
  127.4 10.1 %shard_map.90 = (f32[16,128]{1,0:T(8,128)S(1)}, f32[16,128]{1,0:T(8,128)}) custom-call(s32[1]{0:T(128)} %bitcast.95.count_ref, s32[2,128]{1,0:T(2,128)S(4)} %get-tuple-element.11.pairs, f32[16,128]{1,0:T(8,128)S(1)} %get-tuple-element.12.mass, f32[128,128,128]{2,1,0:T(8,128)S(1)} %get-tuple-element.13.cached, ...), custom_call_target="tpu_custom_call" | custom-call | tf_op jit(solution)/shard_map/pallas_call | solution.py:253
  137.5 1.8 all-gather.3
  139.3 44.8 %all_to_all.28 = f32[16,16,128]{2,1,0:T(8,128)S(1)} all-to-all(f32[16,16,128]{2,1,0:T(8,128)S(1)} %broadcast_in_dim.19), channel_id=1, replica_groups=mesh['z'=16,'c'=2,'y'=4,'x'=4] {'z'}, dimensions={0} | all-to-all | bytes 262144 | tf_op jit(solution)/shard_map/all_to_all | solution.py:278
  184.1 0.7 add_subtract_fusion
  (4 shorter events, 0.1 us)
Async XLA Ops:
  2.1 40.4 %all-to-all-start = ((bf16[16,64,128]{2,1,0:T(8,128)(2,1)}), bf16[16,64,128]{2,1,0:T(8,128)(2,1)S(1)}, u32[]{:S(2)}, u32[]{:S(2)}) async-start(bf16[16,64,128]{2,1,0:T(8,128)(2,1)} %shard_map.86), calls=%async_computation | async-start | bytes 524288 | tf_op jit(solution)/shard_map/all_to_all | solution.py:278

commit v9 on v8

--- a/solution.py
+++ b/solution.py
@@ -17,6 +17,8 @@
 empty_peak = -1e30
 log2e = 1.0 / math.log(2.0)
 to_log2 = log2e / smoothing_epsilon
+gather_first = 10
+sums_first = (2, 0)
 group = 16
 light_group = 8
 pot_most = 20.0
@@ -145,15 +147,9 @@
 
 
 def first_kernel(
-    far_pairs, far_start, far_source_mass, far_target_mass, count_ref, source, target,
-    cached, rows, columns, pairs, source_mass, target_mass, partial,
-    start, arrived, wide_source, wide_target, weights, total, peak, sums,
+    count_ref, pairs, start, source, target, cached, rows, columns, partial,
+    wide_source, wide_target, weights, total, peak, sums,
 ):
-    moves = fetches(
-        (far_pairs, far_start, far_source_mass, far_target_mass),
-        (pairs, start, source_mass, target_mass),
-        arrived,
-    )
     blocks = source.shape[1]
     features = source.shape[2]
     for device in range(source.shape[0]):
@@ -164,16 +160,14 @@
     parts = lines // blocks
     for ring in range(rings):
         for core in range(cores):
-            at = (ring * cores + core) * parts
+            owner = (ring + gather_first) % rings
+            at = (owner * cores + core) * parts
             piece = target[core, ring].astype(jnp.float32)
             wide_target[:, pl.ds(at, parts), :] = piece.reshape(blocks, parts, frames)
     for block in range(blocks):
         rows[block] = wide_source[block].T.astype(jnp.bfloat16)
         columns[block] = wide_target[block].astype(jnp.bfloat16)
 
-    for move in moves[:2]:
-        move.wait()
-
     def kernel_of(slot, source, target):
         value = jnp.exp2(scores(rows[source], columns[target]) * to_log2)
         cached[slot] = value
@@ -183,8 +177,6 @@
         group, count_ref[0], pairs, rows, columns, start, kernel_of,
         weights, total, peak, sums, partial,
     )
-    for move in moves[2:]:
-        move.wait()
 
 
 def column_kernel(
@@ -274,8 +266,11 @@
     return jnp.broadcast_to(x[None], (lax.axis_size(axis), *x.shape))
 
 
-def exchanged(x, axis):
-    return lax.all_to_all(x, axis, 0, 0, tiled=True)
+def exchanged(x, axis, first=0):
+    if not first:
+        return lax.all_to_all(x, axis, 0, 0, tiled=True)
+    order = [(k + first) % x.shape[0] for k in range(x.shape[0])]
+    return lax.all_to_all(x, axis, 0, 0, axis_index_groups=[order], tiled=True)
 
 
 def local_chain(source, target, start, source_mass, target_mass, pairs, count, over_tgt, over_src):
@@ -287,24 +282,21 @@
     many = jax.ShapeDtypeStruct((across, source_blocks, frames), f32)
     square = pltpu.VMEM((source_blocks, frames, frames), f32)
     flat = pltpu.VMEM((source_blocks, frames), f32)
-    listed = pltpu.SMEM(pairs.shape, jnp.int32)
     arrivals = pltpu.SemaphoreType.DMA
-    *kept, pairs, source_mass, target_mass, partial = called(
+    *kept, partial = called(
         first_kernel,
         [
             pltpu.VMEM((slots, frames, frames), f32),
             pltpu.VMEM((source_blocks, frames, features), bf16),
             pltpu.VMEM((target_blocks, features, frames), bf16),
-            listed, flat, flat, many,
+            many,
         ],
         [
-            flat, arrivals((4,)),
             pltpu.VMEM((source_blocks, features, frames), f32),
             pltpu.VMEM((target_blocks, features, frames), f32),
             flat, square, square, flat,
         ],
-        pairs, start, source_mass, target_mass, count, source, target,
-        far=4,
+        count, pairs, start, source, target,
     )
     for iteration in range(ITERS):
         last = iteration == ITERS - 1
@@ -318,7 +310,7 @@
             count, pairs, source_mass, *kept, over_tgt(partial),
         )
         partial, scaling = results[0], results[-1]
-        gathered = over_src(partial)
+        gathered = over_src(partial, sums_first[iteration])
         if not last:
             (partial,) = called(
                 row_kernel,
@@ -330,40 +322,51 @@
     return scaling, potential
 
 
-def over_src(partial):
+def over_src(partial, first):
     both = lax.all_gather(partial, "c")
-    return exchanged(copies(log_sum_exp([both[0], both[1]]), "z"), "z")
-
-
-def copying_kernel(far, copied, near, arrived):
-    (move,) = fetches((far,), (near,), arrived)
-    move.wait()
+    return exchanged(copies(log_sum_exp([both[0], both[1]]), "z"), "z", first)
+
+
+def copying_kernel(far, *refs):
+    small = (len(refs) - 3) // 2
+    copied, near, arrived = refs[2 * small :]
+    moves = fetches((far, *refs[:small]), (near, *refs[small : 2 * small]), arrived)
+    moves[0].wait()
     lines = near[...].astype(jnp.float32).reshape(copied.shape[1:]).astype(copied.dtype)
     copied[...] = jnp.broadcast_to(lines[None], copied.shape)
-
-
-def line_copies(x, axis):
+    for move in moves[1:]:
+        move.wait()
+
+
+def line_copies(x, axis, *small):
     blocks, features, frames = x.shape
     lines = jax.ShapeDtypeStruct((lax.axis_size(axis), blocks * features, frames), x.dtype)
-    (copied,) = called(
+    near = [
+        (pltpu.SMEM if jnp.issubdtype(one.dtype, jnp.integer) else pltpu.VMEM)(one.shape, one.dtype)
+        for one in small
+    ]
+    *near, copied = called(
         copying_kernel,
-        [lines],
-        [pltpu.VMEM(x.shape, x.dtype), pltpu.SemaphoreType.DMA((1,))],
-        x,
-        far=1,
-    )
-    return copied
+        [*near, lines],
+        [pltpu.VMEM(x.shape, x.dtype), pltpu.SemaphoreType.DMA((1 + len(small),))],
+        x, *small,
+        far=1 + len(small),
+    )
+    return copied, near
 
 
 def on_device(
     source_embed, target_embed, source_mass, target_mass, target_start, block_pairs, counts
 ):
     pairs = block_pairs.reshape(block_pairs.shape[2], 2).T
-    columns = exchanged(line_copies(jnp.swapaxes(target_embed, 1, 2), "z"), "z")
+    copied, (pairs, start, source_mass, target_mass) = line_copies(
+        jnp.swapaxes(target_embed, 1, 2), "z", pairs, target_start, source_mass, target_mass
+    )
+    columns = exchanged(copied, "z", gather_first)
     source = lax.all_gather(jnp.swapaxes(source_embed, 1, 2), TGT)
     target = lax.all_gather(columns, "c")
     return local_chain(
-        source, target, target_start, source_mass, target_mass, pairs, counts.reshape(1),
+        source, target, start, source_mass, target_mass, pairs, counts.reshape(1),
         lambda partial: exchanged(partial, TGT), over_src,
     )
 

time: 185 us -> 162 us (0.88)
  the two profiles are of different devices: /device:TPU:32 before, /device:TPU:6 now
where the time goes in v9:
time: 162 us; the launch traced here: 161 us
  blocking collectives  127 us (78%)
  starting transfers between devices  17.1 us (11%)
  Pallas kernels  14.9 us (9%)
    all_to_all x3, blocking collectives, exchanged(): return lax.all_to_all(x, axis, 0, 0, tiled=True)  66.2 us
    all_to_all x1, blocking collectives, exchanged(): return lax.all_to_all(x, axis, 0, 0, axis_index_groups=[order], tiled=True)  31.3 us
    all_gather x1, blocking collectives, on_device(): source = lax.all_gather(jnp.swapaxes(source_embed, 1, 2), TGT)  23.9 us
    all_to_all x1, starting transfers between devices, exchanged(): return lax.all_to_all(x, axis, 0, 0, axis_index_groups=[order], tiled=True)  17.1 us
    pallas_call x5, Pallas kernels, called(): pl.pallas_call(body, out_shape=outs, in_specs=[pl.BlockSpec(memory_space=...  14.9 us
    all_gather x2, blocking collectives, over_src(): both = lax.all_gather(partial, 'c')  3.63 us
  transfers between devices with their start and end apart: 1, of which 0 were waited for; matrix products, arithmetic and copies ran while one was open for 0% of the time, Pallas kernels for 0%

profile of v9, /device:TPU:6, one launch (start us, length us, event | category | flops | bytes accessed | tf_op | source)
XLA Modules:
  0.0 161.3 jit_solution(7155166992285710071)
XLA Ops:
  0.6 1.6 shard_map.86
  2.2 17.1 %all-to-all-start = ((bf16[16,64,128]{2,1,0:T(8,128)(2,1)}), bf16[16,64,128]{2,1,0:T(8,128)(2,1)S(1)}, u32[]{:S(2)}, u32[]{:S(2)}) async-start(bf16[16,64,128]{2,1,0:T(8,128)(2,1)} %get-tuple-element.16), calls=%async_computation | async-start | bytes 524288 | tf_op jit(solution)/shard_map/all_to_all | solution.py:273
  19.9 23.9 %all-gather = bf16[256,8,128]{2,1,0:T(8,128)(2,1)S(1)} all-gather(bf16[16,8,128]{2,1,0:T(8,128)(2,1)} %bitcast.98), channel_id=2, replica_groups=mesh['z'=16,'c'=2,'y'=4,'x'=4] {'y','x'}, dimensions={0}, use_global_device_ids=true | all-gather | bytes 557056 | tf_op jit(solution)/shard_map/all_gather | solution.py:366
  43.8 0.0 all-to-all-done
  43.8 2.2 %all-gather.1 = bf16[32,64,128]{2,1,0:T(8,128)(2,1)S(1)} all-gather(bf16[16,64,128]{2,1,0:T(8,128)(2,1)S(1)} %all-to-all-done), channel_id=3, replica_groups=mesh['z'=16,'c'=2,'y'=4,'x'=4] {'c'}, dimensions={0}, use_global_device_ids=true | all-gather | bytes 786432 | tf_op jit(solution)/shard_map/all_gather | solution.py:367
  46.0 1.7 %shard_map.87 = (f32[128,128,128]{2,1,0:T(8,128)S(1)}, bf16[16,128,128]{2,1,0:T(8,128)(2,1)S(1)}, bf16[16,128,128]{2,1,0:T(8,128)(2,1)S(1)}, f32[16,16,128]{2,1,0:T(8,128)S(1)}) custom-call(s32[1]{0:T(128)} %bitcast.92.count_ref, s32[2,128]{1,0:T(2,128)S(4)} %get-tuple-element.13.pairs, f32[16,128]{1,0:T(8,128)S(1)} %get-tuple-element.15.start, ...), custom_call_target="tpu_custom_call" | custom-call | tf_op jit(solution)/shard_map/pallas_call | solution.py:245
  47.7 17.3 %all_to_all.25.gathered = f32[16,16,128]{2,1,0:T(8,128)S(1)} all-to-all(f32[16,16,128]{2,1,0:T(8,128)S(1)} %get-tuple-element.21), channel_id=1, replica_groups=mesh['z'=16,'c'=2,'y'=4,'x'=4] {'y','x'}, dimensions={0} | all-to-all | bytes 262144 | tf_op jit(solution)/shard_map/all_to_all | solution.py:271
  65.0 5.4 %shard_map.88 = f32[16,128]{1,0:T(8,128)S(1)} custom-call(s32[1]{0:T(128)} %bitcast.93.count_ref, s32[2,128]{1,0:T(2,128)S(4)} %get-tuple-element.13.pairs, f32[16,128]{1,0:T(8,128)S(1)} %get-tuple-element.14.mass, f32[128,128,128]{2,1,0:T(8,128)S(1)} %get-tuple-element.17.cached, bf16[16,128,128]{2,1,0:T(8,128)(2,1)S(1)} %get-tuple-element.18.rows, ...), custom_call_target="tpu_custom_call" | custom-call | tf_op jit(solution)/shard_map/pallas_call | solution.py:245
  70.4 1.8 %all-gather.2 = f32[32,128]{1,0:T(8,128)S(1)} all-gather(f32[16,128]{1,0:T(8,128)S(1)} %shard_map.88), channel_id=4, replica_groups=mesh['z'=16,'c'=2,'y'=4,'x'=4] {'c'}, dimensions={0}, use_global_device_ids=true | all-gather | bytes 24576 | tf_op jit(solution)/shard_map/all_gather | solution.py:326
  72.2 31.3 %all_to_all.26.gathered = f32[16,16,128]{2,1,0:T(8,128)S(1)} all-to-all(f32[16,16,128]{2,1,0:T(8,128)S(1)} %broadcast_in_dim.17), channel_id=1, replica_groups={{64,96,128,160,192,224,256,288,320,352,384,416,448,480,0,32},{65,97,129..., dimensions={0} | all-to-all | bytes 262144 | tf_op jit(solution)/shard_map/all_to_all | solution.py:273
  103.5 0.8 shard_map.89
  104.4 17.7 %all_to_all.27.gathered = f32[16,16,128]{2,1,0:T(8,128)S(1)} all-to-all(f32[16,16,128]{2,1,0:T(8,128)S(1)} %shard_map.89), channel_id=1, replica_groups=mesh['z'=16,'c'=2,'y'=4,'x'=4] {'y','x'}, dimensions={0} | all-to-all | bytes 262144 | tf_op jit(solution)/shard_map/all_to_all | solution.py:271
  122.1 5.4 %shard_map.90 = (f32[16,128]{1,0:T(8,128)S(1)}, f32[16,128]{1,0:T(8,128)}) custom-call(s32[1]{0:T(128)} %bitcast.95.count_ref, s32[2,128]{1,0:T(2,128)S(4)} %get-tuple-element.13.pairs, f32[16,128]{1,0:T(8,128)S(1)} %get-tuple-element.14.mass, f32[128,128,128]{2,1,0:T(8,128)S(1)} %get-tuple-element.17.cached, ...), custom_call_target="tpu_custom_call" | custom-call | tf_op jit(solution)/shard_map/pallas_call | solution.py:245
  127.5 1.8 %all-gather.3 = f32[32,128]{1,0:T(8,128)S(1)} all-gather(f32[16,128]{1,0:T(8,128)S(1)} %get-tuple-element.23), channel_id=5, replica_groups=mesh['z'=16,'c'=2,'y'=4,'x'=4] {'c'}, dimensions={0}, use_global_device_ids=true | all-gather | bytes 24576 | tf_op jit(solution)/shard_map/all_gather | solution.py:326
  129.4 31.2 %all_to_all.28 = f32[16,16,128]{2,1,0:T(8,128)S(1)} all-to-all(f32[16,16,128]{2,1,0:T(8,128)S(1)} %broadcast_in_dim.19), channel_id=1, replica_groups=mesh['z'=16,'c'=2,'y'=4,'x'=4] {'z'}, dimensions={0} | all-to-all | bytes 262144 | tf_op jit(solution)/shard_map/all_to_all | solution.py:271
  160.6 0.7 add_subtract_fusion
  (4 shorter events, 0.1 us)
Async XLA Ops:
  2.2 41.6 %all-to-all-start = ((bf16[16,64,128]{2,1,0:T(8,128)(2,1)}), bf16[16,64,128]{2,1,0:T(8,128)(2,1)S(1)}, u32[]{:S(2)}, u32[]{:S(2)}) async-start(bf16[16,64,128]{2,1,0:T(8,128)(2,1)} %get-tuple-element.16), calls=%async_computation | async-start | bytes 524288 | tf_op jit(solution)/shard_map/all_to_all | solution.py:273

commit v10 on v9

--- a/solution.py
+++ b/solution.py
@@ -18,7 +18,7 @@
 log2e = 1.0 / math.log(2.0)
 to_log2 = log2e / smoothing_epsilon
 gather_first = 10
-sums_first = (2, 0)
+sums_first = (2, 2)
 group = 16
 light_group = 8
 pot_most = 20.0

time: 162 us -> 203 us (1.25)
  the two profiles are of different devices: /device:TPU:6 before, /device:TPU:32 now
where the time goes in v10:
time: 203 us; the launch traced here: 202 us
  blocking collectives  170 us (84%)
  starting transfers between devices  16.6 us (8%)
  Pallas kernels  13.5 us (7%)
    all_to_all x2, blocking collectives, exchanged(): return lax.all_to_all(x, axis, 0, 0, axis_index_groups=[order], tiled=True)  114 us
    all_to_all x2, blocking collectives, exchanged(): return lax.all_to_all(x, axis, 0, 0, tiled=True)  25.3 us
    all_gather x1, blocking collectives, on_device(): source = lax.all_gather(jnp.swapaxes(source_embed, 1, 2), TGT)  24.4 us
    all_to_all x1, starting transfers between devices, exchanged(): return lax.all_to_all(x, axis, 0, 0, axis_index_groups=[order], tiled=True)  16.6 us
    pallas_call x5, Pallas kernels, called(): pl.pallas_call(body, out_shape=outs, in_specs=[pl.BlockSpec(memory_space=...  13.5 us
  transfers between devices with their start and end apart: 1, of which 0 were waited for; matrix products, arithmetic and copies ran while one was open for 0% of the time, Pallas kernels for 0%

profile of v10, /device:TPU:32, one launch (start us, length us, event | category | flops | bytes accessed | tf_op | source)
XLA Modules:
  0.0 202.0 jit_solution(5113390005001076596)
XLA Ops:
  0.6 1.6 shard_map.86
  2.2 16.6 %all-to-all-start = ((bf16[16,64,128]{2,1,0:T(8,128)(2,1)}), bf16[16,64,128]{2,1,0:T(8,128)(2,1)S(1)}, u32[]{:S(2)}, u32[]{:S(2)}) async-start(bf16[16,64,128]{2,1,0:T(8,128)(2,1)} %get-tuple-element.16), calls=%async_computation | async-start | bytes 524288 | tf_op jit(solution)/shard_map/all_to_all | solution.py:273
  19.5 24.4 %all-gather = bf16[256,8,128]{2,1,0:T(8,128)(2,1)S(1)} all-gather(bf16[16,8,128]{2,1,0:T(8,128)(2,1)} %bitcast.98), channel_id=2, replica_groups=mesh['z'=16,'c'=2,'y'=4,'x'=4] {'y','x'}, dimensions={0}, use_global_device_ids=true | all-gather | bytes 557056 | tf_op jit(solution)/shard_map/all_gather | solution.py:366
  43.8 0.0 all-to-all-done
  43.8 2.2 %all-gather.1 = bf16[32,64,128]{2,1,0:T(8,128)(2,1)S(1)} all-gather(bf16[16,64,128]{2,1,0:T(8,128)(2,1)S(1)} %all-to-all-done), channel_id=3, replica_groups=mesh['z'=16,'c'=2,'y'=4,'x'=4] {'c'}, dimensions={0}, use_global_device_ids=true | all-gather | bytes 786432 | tf_op jit(solution)/shard_map/all_gather | solution.py:367
  46.0 1.7 shard_map.87
  47.7 14.7 %all_to_all.25.gathered = f32[16,16,128]{2,1,0:T(8,128)S(1)} all-to-all(f32[16,16,128]{2,1,0:T(8,128)S(1)} %get-tuple-element.21), channel_id=1, replica_groups=mesh['z'=16,'c'=2,'y'=4,'x'=4] {'y','x'}, dimensions={0} | all-to-all | bytes 262144 | tf_op jit(solution)/shard_map/all_to_all | solution.py:271
  62.4 4.7 %shard_map.88 = f32[16,128]{1,0:T(8,128)S(1)} custom-call(s32[1]{0:T(128)} %bitcast.93.count_ref, s32[2,128]{1,0:T(2,128)S(4)} %get-tuple-element.13.pairs, f32[16,128]{1,0:T(8,128)S(1)} %get-tuple-element.14.mass, f32[128,128,128]{2,1,0:T(8,128)S(1)} %get-tuple-element.17.cached, bf16[16,128,128]{2,1,0:T(8,128)(2,1)S(1)} %get-tuple-element.18.rows, ...), custom_call_target="tpu_custom_call" | custom-call | tf_op jit(solution)/shard_map/pallas_call | solution.py:245
  67.2 1.8 all-gather.2
  69.0 56.0 %all_to_all.26.gathered = f32[16,16,128]{2,1,0:T(8,128)S(1)} all-to-all(f32[16,16,128]{2,1,0:T(8,128)S(1)} %broadcast_in_dim.17), channel_id=1, replica_groups={{64,96,128,160,192,224,256,288,320,352,384,416,448,480,0,32},{65,97,129..., dimensions={0} | all-to-all | bytes 262144 | tf_op jit(solution)/shard_map/all_to_all | solution.py:273
  125.1 0.8 shard_map.89
  125.8 10.6 %all_to_all.27.gathered = f32[16,16,128]{2,1,0:T(8,128)S(1)} all-to-all(f32[16,16,128]{2,1,0:T(8,128)S(1)} %shard_map.89), channel_id=1, replica_groups=mesh['z'=16,'c'=2,'y'=4,'x'=4] {'y','x'}, dimensions={0} | all-to-all | bytes 262144 | tf_op jit(solution)/shard_map/all_to_all | solution.py:271
  136.4 4.7 %shard_map.90 = (f32[16,128]{1,0:T(8,128)S(1)}, f32[16,128]{1,0:T(8,128)}) custom-call(s32[1]{0:T(128)} %bitcast.95.count_ref, s32[2,128]{1,0:T(2,128)S(4)} %get-tuple-element.13.pairs, f32[16,128]{1,0:T(8,128)S(1)} %get-tuple-element.14.mass, f32[128,128,128]{2,1,0:T(8,128)S(1)} %get-tuple-element.17.cached, ...), custom_call_target="tpu_custom_call" | custom-call | tf_op jit(solution)/shard_map/pallas_call | solution.py:245
  141.1 1.8 all-gather.3
  143.0 58.4 %all_to_all.28 = f32[16,16,128]{2,1,0:T(8,128)S(1)} all-to-all(f32[16,16,128]{2,1,0:T(8,128)S(1)} %broadcast_in_dim.19), channel_id=1, replica_groups={{64,96,128,160,192,224,256,288,320,352,384,416,448,480,0,32},{65,97,129..., dimensions={0} | all-to-all | bytes 262144 | tf_op jit(solution)/shard_map/all_to_all | solution.py:273
  201.3 0.7 add_subtract_fusion
  (4 shorter events, 0.1 us)
Async XLA Ops:
  2.2 41.6 %all-to-all-start = ((bf16[16,64,128]{2,1,0:T(8,128)(2,1)}), bf16[16,64,128]{2,1,0:T(8,128)(2,1)S(1)}, u32[]{:S(2)}, u32[]{:S(2)}) async-start(bf16[16,64,128]{2,1,0:T(8,128)(2,1)} %get-tuple-element.16), calls=%async_computation | async-start | bytes 524288 | tf_op jit(solution)/shard_map/all_to_all | solution.py:273

commit v11 on v7

--- a/solution.py
+++ b/solution.py
@@ -11,12 +11,13 @@
 
 ITERS = 2
 SRC = ("z", "c")
-TGT = ("y", "x")
 
 smoothing_epsilon = 4.0
 empty_peak = -1e30
 log2e = 1.0 / math.log(2.0)
 to_log2 = log2e / smoothing_epsilon
+ring_first = 10
+across_first = 10
 group = 16
 light_group = 8
 pot_most = 20.0
@@ -154,8 +155,10 @@
         arrived,
     )
     features = source.shape[2]
-    for device in range(source.shape[0]):
-        wide[:, pl.ds(device * features, features), :] = source[device].astype(jnp.float32)
+    across = source.shape[0]
+    for device in range(across):
+        at = (device + across_first) % across * features
+        wide[:, pl.ds(at, features), :] = source[device].astype(jnp.float32)
     for block in range(source.shape[1]):
         rows[block] = wide[block].T.astype(rows.dtype)
     for move in moves:
@@ -171,7 +174,8 @@
     parts = lines // blocks
     for ring in range(rings):
         for core in range(cores):
-            at = (ring * cores + core) * parts
+            owner = (ring + ring_first) % rings
+            at = (owner * cores + core) * parts
             piece = target[core, ring].astype(jnp.float32)
             wide[:, pl.ds(at, parts), :] = piece.reshape(blocks, parts, frames)
     for block in range(blocks):
@@ -275,8 +279,9 @@
     return jnp.broadcast_to(x[None], (lax.axis_size(axis), *x.shape))
 
 
-def exchanged(x, axis):
-    return lax.all_to_all(x, axis, 0, 0, tiled=True)
+def exchanged(x, axis, first):
+    order = [(k + first) % x.shape[0] for k in range(x.shape[0])]
+    return lax.all_to_all(x, axis, 0, 0, axis_index_groups=[order], tiled=True)
 
 
 def local_chain(source, target, start, source_mass, target_mass, pairs, count, over_tgt, over_src):
@@ -337,7 +342,7 @@
 
 def over_src(partial):
     both = lax.all_gather(partial, "c")
-    return exchanged(copies(log_sum_exp([both[0], both[1]]), "z"), "z")
+    return exchanged(copies(log_sum_exp([both[0], both[1]]), "z"), "z", ring_first)
 
 
 def copying_kernel(source, target, sources, targets, near_source, near_target, arrived):
@@ -350,7 +355,7 @@
 
 
 def copies_of_both(source, target):
-    across, rings = lax.axis_size(TGT), lax.axis_size("z")
+    across, rings = lax.axis_size("tgt"), lax.axis_size("z")
     lines = target.shape[0] * target.shape[1]
     return pl.pallas_call(
         copying_kernel,
@@ -375,29 +380,29 @@
     sources, targets = copies_of_both(
         jnp.swapaxes(source_embed, 1, 2), jnp.swapaxes(target_embed, 1, 2)
     )
-    source = exchanged(sources, TGT)
-    target = lax.all_gather(exchanged(targets, "z"), "c")
+    source = exchanged(sources, "tgt", across_first)
+    target = lax.all_gather(exchanged(targets, "z", ring_first), "c")
     return local_chain(
         source, target, target_start, source_mass, target_mass, pairs, counts.reshape(1),
-        lambda partial: exchanged(partial, TGT), over_src,
+        lambda partial: exchanged(partial, "tgt", across_first), over_src,
     )
 
 
 def solution(mesh):
-    split = Mesh(mesh.devices.reshape(16, 2, 4, 4), (*SRC, *TGT))
+    split = Mesh(mesh.devices.reshape(16, 2, 16), (*SRC, "tgt"))
     placed = (
-        P(SRC, None, TGT),
-        P(TGT, None, SRC),
+        P(SRC, None, "tgt"),
+        P("tgt", None, SRC),
         P(SRC, None),
-        P(TGT, None),
-        P(TGT, None),
-        P(SRC, TGT, None, None),
-        P(SRC, TGT),
+        P("tgt", None),
+        P("tgt", None),
+        P(SRC, "tgt", None, None),
+        P(SRC, "tgt"),
     )
     return jax.shard_map(
         on_device,
         mesh=split,
         in_specs=placed,
-        out_specs=(P(SRC, None), P(TGT, None)),
+        out_specs=(P(SRC, None), P("tgt", None)),
         check_vma=False,
     )

time: 173 us -> 206 us (1.19)
  the two profiles are of different devices: /device:TPU:8 before, /device:TPU:4 now
where the time goes in v11:
time: 206 us; the launch traced here: 205 us
  blocking collectives  148 us (72%)
  Pallas kernels  29.6 us (14%)
  starting transfers between devices  14.8 us (7%)
  waiting for transfers between devices  10.8 us (5%)
    all_to_all x5, blocking collectives, exchanged(): return lax.all_to_all(x, axis, 0, 0, axis_index_groups=[order], tiled=True)  142 us
    pallas_call x5, Pallas kernels, called(): pl.pallas_call(body, out_shape=outs, in_specs=[pl.BlockSpec(memory_space=...  28 us
    all_to_all x1, starting transfers between devices, exchanged(): return lax.all_to_all(x, axis, 0, 0, axis_index_groups=[order], tiled=True)  14.8 us
    all_to_all x1, waiting for transfers between devices, exchanged(): return lax.all_to_all(x, axis, 0, 0, axis_index_groups=[order], tiled=True)  10.8 us
  transfers between devices with their start and end apart: 1, of which 1 were waited for; matrix products, arithmetic and copies ran while one was open for 0% of the time, Pallas kernels for 0%

profile of v11, /device:TPU:4, one launch (start us, length us, event | category | flops | bytes accessed | tf_op | source)
XLA Modules:
  0.0 205.3 jit_solution(17912625926832280494)
XLA Ops:
  0.6 1.6 shard_map.86
  2.2 17.4 %all_to_all.30.source = bf16[16,16,8,128]{3,2,1,0:T(8,128)(2,1)S(1)} all-to-all(bf16[16,16,8,128]{3,2,1,0:T(8,128)(2,1)S(1)} %get-tuple-element.14), channel_id=1, replica_groups={{10,11,12,13,14,15,0,1,2,3,4,5,6,7,8,9},{26,27,28,29,30,31,16,17,18,19,..., dimensions={0} | all-to-all | bytes 1048576 | tf_op jit(solution)/shard_map/all_to_all | solution.py:284
  19.7 14.8 %all-to-all-start.1 = ((bf16[16,64,128]{2,1,0:T(8,128)(2,1)}), bf16[16,64,128]{2,1,0:T(8,128)(2,1)S(1)}, u32[]{:S(2)}, u32[]{:S(2)}) async-start(bf16[16,64,128]{2,1,0:T(8,128)(2,1)} %get-tuple-element.19), calls=%async_computation.1 | async-start | bytes 524288 | tf_op jit(solution)/shard_map/all_to_all | solution.py:284
  35.1 0.8 shard_map.87
  35.9 10.8 %all-to-all-done.1 = bf16[16,64,128]{2,1,0:T(8,128)(2,1)S(1)} async-done(((bf16[16,64,128]{2,1,0:T(8,128)(2,1)}), bf16[16,64,128]{2,1,0:T(8,128)(2,1)S(1)}, u32[]{:S(2)}, u32[]{:S(2)}) %all-to-all-start.1) | async-done | bytes 262176 | tf_op jit(solution)/shard_map/all_to_all | solution.py:284
  46.7 2.2 %all-gather = bf16[32,64,128]{2,1,0:T(8,128)(2,1)S(1)} all-gather(bf16[16,64,128]{2,1,0:T(8,128)(2,1)S(1)} %all-to-all-done.1), channel_id=2, replica_groups=mesh['z'=16,'c'=2,'tgt'=16] {'c'}, dimensions={0}, use_global_device_ids=true | all-gather | bytes 786432 | tf_op jit(solution)/shard_map/all_gather | solution.py:384
  48.9 2.2 %shard_map.88 = (f32[128,128,128]{2,1,0:T(8,128)S(1)}, bf16[16,128,128]{2,1,0:T(8,128)(2,1)S(1)}, f32[16,16,128]{2,1,0:T(8,128)S(1)}) custom-call(s32[1]{0:T(128)} %bitcast.91.count_ref, s32[2,128]{1,0:T(2,128)S(4)} %get-tuple-element.15.pairs, f32[16,128]{1,0:T(8,128)S(1)} %get-tuple-element.17.start, bf16[16,128,128]{2,1,0:T(8,128)(2,1)S(1)} %get-tuple-element.18.rows, ...), custom_call_target="tpu_custom_call" | custom-call | tf_op jit(solution)/shard_map/pallas_call | solution.py:258
  51.1 27.3 %all_to_all.31.gathered = f32[16,16,128]{2,1,0:T(8,128)S(1)} all-to-all(f32[16,16,128]{2,1,0:T(8,128)S(1)} %get-tuple-element.23), channel_id=1, replica_groups={{10,11,12,13,14,15,0,1,2,3,4,5,6,7,8,9},{26,27,28,29,30,31,16,17,18,19,..., dimensions={0} | all-to-all | bytes 262144 | tf_op jit(solution)/shard_map/all_to_all | solution.py:284
  78.4 12.0 %shard_map.89 = f32[16,128]{1,0:T(8,128)S(1)} custom-call(s32[1]{0:T(128)} %bitcast.92.count_ref, s32[2,128]{1,0:T(2,128)S(4)} %get-tuple-element.15.pairs, f32[16,128]{1,0:T(8,128)S(1)} %get-tuple-element.16.mass, f32[128,128,128]{2,1,0:T(8,128)S(1)} %get-tuple-element.20.cached, bf16[16,128,128]{2,1,0:T(8,128)(2,1)S(1)} %get-tuple-element.18.rows, ...), custom_call_target="tpu_custom_call" | custom-call | tf_op jit(solution)/shard_map/pallas_call | solution.py:258
  90.3 1.8 all-gather.1
  92.2 35.7 %all_to_all.32.gathered = f32[16,16,128]{2,1,0:T(8,128)S(1)} all-to-all(f32[16,16,128]{2,1,0:T(8,128)S(1)} %broadcast_in_dim.17), channel_id=1, replica_groups={{320,352,384,416,448,480,0,32,64,96,128,160,192,224,256,288},{321,353,3..., dimensions={0} | all-to-all | bytes 262144 | tf_op jit(solution)/shard_map/all_to_all | solution.py:284
  127.8 1.1 shard_map.90
  129.0 22.4 %all_to_all.33.gathered = f32[16,16,128]{2,1,0:T(8,128)S(1)} all-to-all(f32[16,16,128]{2,1,0:T(8,128)S(1)} %shard_map.90), channel_id=1, replica_groups={{10,11,12,13,14,15,0,1,2,3,4,5,6,7,8,9},{26,27,28,29,30,31,16,17,18,19,..., dimensions={0} | all-to-all | bytes 262144 | tf_op jit(solution)/shard_map/all_to_all | solution.py:284
  151.4 12.0 %shard_map.91 = (f32[16,128]{1,0:T(8,128)S(1)}, f32[16,128]{1,0:T(8,128)}) custom-call(s32[1]{0:T(128)} %bitcast.94.count_ref, s32[2,128]{1,0:T(2,128)S(4)} %get-tuple-element.15.pairs, f32[16,128]{1,0:T(8,128)S(1)} %get-tuple-element.16.mass, f32[128,128,128]{2,1,0:T(8,128)S(1)} %get-tuple-element.20.cached, ...), custom_call_target="tpu_custom_call" | custom-call | tf_op jit(solution)/shard_map/pallas_call | solution.py:258
  163.3 1.8 all-gather.2
  165.2 39.5 %all_to_all.34 = f32[16,16,128]{2,1,0:T(8,128)S(1)} all-to-all(f32[16,16,128]{2,1,0:T(8,128)S(1)} %broadcast_in_dim.19), channel_id=1, replica_groups={{320,352,384,416,448,480,0,32,64,96,128,160,192,224,256,288},{321,353,3..., dimensions={0} | all-to-all | bytes 262144 | tf_op jit(solution)/shard_map/all_to_all | solution.py:284
  204.7 0.7 add_subtract_fusion
  (4 shorter events, 0.1 us)
Async XLA Ops:
  19.7 27.0 %all-to-all-start.1 = ((bf16[16,64,128]{2,1,0:T(8,128)(2,1)}), bf16[16,64,128]{2,1,0:T(8,128)(2,1)S(1)}, u32[]{:S(2)}, u32[]{:S(2)}) async-start(bf16[16,64,128]{2,1,0:T(8,128)(2,1)} %get-tuple-element.19), calls=%async_computation.1 | async-start | bytes 524288 | tf_op jit(solution)/shard_map/all_to_all | solution.py:284
